TPU v7x, 32 devices: a whole 2x2x4 slice. The times are simulated.
32 devices in a mesh: section: 2 (over core), dp: 16 (over z, y, x).
Axes of the slice: x: 2, y: 2, z: 4, core: 2. Of those that a mesh axis runs over, the one named last changes fastest.
Arguments:
- ends_in: bfloat16 [2, 32, 197, 384], P('section', 'dp'), may hold values from -6 to 6
- vectors: bfloat16 [2, 8, 384], P('section', None, 'dp'), may hold values from -1 to 1
- up_bias: bfloat16 [2, 1536], P('section', 'dp'), may hold values from -2 to 2
- w_qkv: bfloat16 [2, 384, 1152], P('section', 'dp'), may hold values from -0.3125 to 0.3125
- w_out: bfloat16 [2, 384, 384], P('section', 'dp'), may hold values from -0.875 to 0.875
- w_up: bfloat16 [2, 384, 1536], P('section', 'dp'), may hold values from -0.3125 to 0.3125
- w_down: bfloat16 [2, 1536, 384], P('section', 'dp'), may hold values from -0.15625 to 0.15625
Outputs:
- ends: bfloat16 [2, 32, 197, 384], P('section', 'dp')
- vectors_grad: float32 [2, 8, 384], P('section', None, 'dp')
- up_bias_grad: float32 [2, 1536], P('section', 'dp')
- w_qkv_grad: float32 [2, 384, 1152], P('section', 'dp')
- w_out_grad: float32 [2, 384, 384], P('section', 'dp')
- w_up_grad: float32 [2, 384, 1536], P('section', 'dp')
- w_down_grad: float32 [2, 1536, 384], P('section', 'dp')
All inputs are finite; a program needn't handle non-finite values.
Results may differ from a plain program's by a relative error of at most 0.012.
Values may be sent and summed in bfloat16 or wider, within the bound.
A program may use at most 128 MiB of HBM per device.

v0:
```python
import jax
import jax.numpy as jnp
from jax import lax
from jax.sharding import PartitionSpec as P

HEADS = 6
HEAD_DIM = 64
MICRO = 2


norm_eps = 1e-06


def passed_along(value, axis, steps):
    count = lax.axis_size(axis)
    first, last = (max(0, -steps), min(count, count - steps))
    return lax.ppermute(value, axis, [(source, source + steps) for source in range(first, last)])


def layer_norm(values, gain_raw, shift_vec):
    average = jnp.mean(values, axis=-1, keepdims=True)
    centered = values - average
    variance = jnp.mean(centered * centered, axis=-1, keepdims=True)
    return centered * lax.rsqrt(variance + norm_eps) * (1.0 + gain_raw) + shift_vec


def smooth_gate(values):
    return jax.nn.gelu(values, approximate=False)


def forward_layer(inputs_low, weight_set, per_micro, seq_len):
    vector_set, up_bias_all, qkv_all, out_all, up_all, down_all = weight_set
    params = vector_set.astype(jnp.float32)
    hidden = inputs_low.astype(jnp.float32)
    normed = layer_norm(hidden, params[0], params[1]).astype(jnp.bfloat16)
    zero_bias = jnp.zeros_like(params[2])
    projected = jnp.dot(normed, qkv_all, preferred_element_type=jnp.float32) + jnp.concatenate(
        [params[2], zero_bias, params[3]]
    )
    projected = projected.astype(jnp.bfloat16)
    head_view = projected.reshape(per_micro, seq_len, 3, HEADS, HEAD_DIM)
    queries = head_view[:, :, 0]
    key_heads = head_view[:, :, 1]
    value_heads = head_view[:, :, 2]
    scores = jnp.einsum(
        "bqhd,bkhd->bhqk", queries, key_heads, preferred_element_type=jnp.float32
    ) * HEAD_DIM ** (-0.5)
    row_max = jnp.max(scores, axis=-1, keepdims=True)
    shifted = jnp.exp(scores - row_max)
    row_total = jnp.sum(shifted, axis=-1, keepdims=True)
    log_total = row_max + jnp.log(row_total)
    probs_low = (shifted / row_total).astype(jnp.bfloat16)
    attended = jnp.einsum(
        "bhqk,bkhd->bqhd", probs_low, value_heads, preferred_element_type=jnp.float32
    )
    attended = attended.reshape(per_micro * seq_len, HEADS * HEAD_DIM).astype(jnp.bfloat16)
    middle = hidden + jnp.dot(attended, out_all, preferred_element_type=jnp.float32) + params[4]
    normed_two = layer_norm(middle, params[5], params[6]).astype(jnp.bfloat16)
    pre_gate = jnp.dot(normed_two, up_all, preferred_element_type=jnp.float32) + up_bias_all.astype(
        jnp.float32
    )
    activated = smooth_gate(pre_gate).astype(jnp.bfloat16)
    outcome = middle + jnp.dot(activated, down_all, preferred_element_type=jnp.float32) + params[7]
    saved_set = (inputs_low, normed, projected, log_total, attended, middle, normed_two, pre_gate)
    return (outcome, saved_set)


def backward_layer(grad_out, saved_set, weight_set, per_micro, seq_len):
    vector_set, up_bias_all, qkv_all, out_all, up_all, down_all = weight_set
    inputs_low, normed, projected, log_total, attended, middle, normed_two, pre_gate = saved_set
    params = vector_set.astype(jnp.float32)
    hidden = inputs_low.astype(jnp.float32)
    model_width = HEADS * HEAD_DIM
    row_count = per_micro * seq_len
    grad_branch = grad_out.astype(jnp.bfloat16)
    grad_down_bias = jnp.sum(grad_branch.astype(jnp.float32), axis=0)
    activated_full, gate_pull = jax.vjp(smooth_gate, pre_gate)
    activated = activated_full.astype(jnp.bfloat16)
    grad_down = jnp.einsum("rf,rd->fd", activated, grad_branch, preferred_element_type=jnp.float32)
    grad_act = jnp.einsum("rd,fd->rf", grad_branch, down_all, preferred_element_type=jnp.float32)
    grad_pre = gate_pull(grad_act)[0].astype(jnp.bfloat16)
    grad_up_bias = jnp.sum(grad_pre.astype(jnp.float32), axis=0)
    grad_up = jnp.einsum("rd,rf->df", normed_two, grad_pre, preferred_element_type=jnp.float32)
    grad_normed_two = jnp.einsum("rf,df->rd", grad_pre, up_all, preferred_element_type=jnp.float32)
    _, second_pull = jax.vjp(layer_norm, middle, params[5], params[6])
    grad_mid_norm, grad_gain_two, grad_shift_two = second_pull(grad_normed_two)
    grad_middle = grad_out + grad_mid_norm
    grad_attn_out = grad_middle.astype(jnp.bfloat16)
    grad_out_bias = jnp.sum(grad_attn_out.astype(jnp.float32), axis=0)
    grad_out_w = jnp.einsum(
        "rd,re->de", attended, grad_attn_out, preferred_element_type=jnp.float32
    )
    grad_attended = jnp.einsum(
        "re,de->rd", grad_attn_out, out_all, preferred_element_type=jnp.float32
    )
    grad_attended = grad_attended.astype(jnp.bfloat16).reshape(per_micro, seq_len, HEADS, HEAD_DIM)
    head_view = projected.reshape(per_micro, seq_len, 3, HEADS, HEAD_DIM)
    queries = head_view[:, :, 0]
    key_heads = head_view[:, :, 1]
    value_heads = head_view[:, :, 2]
    score_scale = HEAD_DIM ** (-0.5)
    scores = (
        jnp.einsum("bqhd,bkhd->bhqk", queries, key_heads, preferred_element_type=jnp.float32)
        * score_scale
    )
    probs_full = jnp.exp(scores - log_total)
    probs_low = probs_full.astype(jnp.bfloat16)
    grad_probs = jnp.einsum(
        "bqhd,bkhd->bhqk", grad_attended, value_heads, preferred_element_type=jnp.float32
    )
    grad_values = jnp.einsum(
        "bhqk,bqhd->bkhd", probs_low, grad_attended, preferred_element_type=jnp.float32
    )
    grad_scores = probs_full * (
        grad_probs - jnp.sum(probs_full * grad_probs, axis=-1, keepdims=True)
    )
    grad_scores = grad_scores.astype(jnp.bfloat16)
    grad_queries = (
        jnp.einsum("bhqk,bkhd->bqhd", grad_scores, key_heads, preferred_element_type=jnp.float32)
        * score_scale
    )
    grad_keys = (
        jnp.einsum("bhqk,bqhd->bkhd", grad_scores, queries, preferred_element_type=jnp.float32)
        * score_scale
    )
    grad_projected = jnp.stack([grad_queries, grad_keys, grad_values], axis=2)
    grad_projected = grad_projected.reshape(row_count, 3 * model_width).astype(jnp.bfloat16)
    grad_bias_all = jnp.sum(grad_projected.astype(jnp.float32), axis=0)
    grad_qkv = jnp.einsum("rd,re->de", normed, grad_projected, preferred_element_type=jnp.float32)
    grad_normed = jnp.einsum(
        "re,de->rd", grad_projected, qkv_all, preferred_element_type=jnp.float32
    )
    _, first_pull = jax.vjp(layer_norm, hidden, params[0], params[1])
    grad_hid_norm, grad_gain_one, grad_shift_one = first_pull(grad_normed)
    grad_hidden = grad_middle + grad_hid_norm
    grad_vectors = jnp.stack(
        [
            grad_gain_one,
            grad_shift_one,
            grad_bias_all[:model_width],
            grad_bias_all[2 * model_width :],
            grad_out_bias,
            grad_gain_two,
            grad_shift_two,
            grad_down_bias,
        ]
    )
    return (grad_hidden, (grad_vectors, grad_up_bias, grad_qkv, grad_out_w, grad_up, grad_down))


def shards(ends_in, vectors, up_bias, w_qkv, w_out, w_up, w_down):
    section_id = lax.axis_index("section")
    is_first = section_id == 0
    local_part = ends_in[0]
    image_count, seq_len, model_width = local_part.shape
    per_micro = image_count // MICRO
    row_count = per_micro * seq_len
    tick_total = MICRO + 1
    gathered = (
        lax.all_gather(vectors[0], "dp", axis=1, tiled=True),
        lax.all_gather(up_bias[0], "dp", axis=0, tiled=True),
        lax.all_gather(w_qkv[0], "dp", axis=0, tiled=True),
        lax.all_gather(w_out[0], "dp", axis=0, tiled=True),
        lax.all_gather(w_up[0], "dp", axis=0, tiled=True),
        lax.all_gather(w_down[0], "dp", axis=0, tiled=True),
    )
    zero_rows = jnp.zeros((row_count, model_width), jnp.bfloat16)
    received = zero_rows
    saved_list = []
    output_rows = []
    for tick_no in range(tick_total):
        if tick_no < MICRO:
            own_rows = local_part[tick_no * per_micro : (tick_no + 1) * per_micro].reshape(
                row_count, model_width
            )
        else:
            own_rows = zero_rows
        layer_in = jnp.where(is_first, own_rows, received)
        result_rows, saved_set = forward_layer(layer_in, gathered, per_micro, seq_len)
        result_low = result_rows.astype(jnp.bfloat16)
        saved_list.append(saved_set)
        output_rows.append(result_low)
        if tick_no < MICRO:
            received = passed_along(result_low, "section", 1)
    saved_stack = jax.tree.map(lambda *arrays: jnp.stack(arrays), *saved_list)
    back_weights = (
        lax.all_gather(vectors[0], "dp", axis=1, tiled=True),
        lax.all_gather(up_bias[0], "dp", axis=0, tiled=True),
        lax.all_gather(w_qkv[0], "dp", axis=0, tiled=True),
        lax.all_gather(w_out[0], "dp", axis=0, tiled=True),
        lax.all_gather(w_up[0], "dp", axis=0, tiled=True),
        lax.all_gather(w_down[0], "dp", axis=0, tiled=True),
    )
    totals = tuple((jnp.zeros(whole_item.shape, jnp.float32) for whole_item in gathered))
    grad_received = zero_rows
    grad_rows = []
    for tick_no in range(tick_total):
        if tick_no < MICRO:
            cot_rows = local_part[tick_no * per_micro : (tick_no + 1) * per_micro].reshape(
                row_count, model_width
            )
        else:
            cot_rows = zero_rows
        grad_in = jnp.where(is_first, grad_received, cot_rows).astype(jnp.float32)
        kept_index = jnp.clip(tick_no - 1 + 2 * section_id, 0, MICRO)
        saved_set = jax.tree.map(
            lambda stacked_item: lax.dynamic_index_in_dim(
                stacked_item, kept_index, 0, keepdims=False
            ),
            saved_stack,
        )
        grad_hidden, grad_terms = backward_layer(
            grad_in, saved_set, back_weights, per_micro, seq_len
        )
        grad_low = grad_hidden.astype(jnp.bfloat16)
        grad_rows.append(grad_low)
        totals = tuple((running + grad_term for running, grad_term in zip(totals, grad_terms)))
        if tick_no < MICRO:
            grad_received = passed_along(grad_low, "section", -1)
    finals = (
        lax.psum_scatter(totals[0], "dp", scatter_dimension=1, tiled=True),
        lax.psum_scatter(totals[1], "dp", scatter_dimension=0, tiled=True),
        lax.psum_scatter(totals[2], "dp", scatter_dimension=0, tiled=True),
        lax.psum_scatter(totals[3], "dp", scatter_dimension=0, tiled=True),
        lax.psum_scatter(totals[4], "dp", scatter_dimension=0, tiled=True),
        lax.psum_scatter(totals[5], "dp", scatter_dimension=0, tiled=True),
    )
    pieces = [
        jnp.where(is_first, grad_rows[tick_no], output_rows[tick_no])
        for tick_no in range(1, tick_total)
    ]
    ends = jnp.concatenate(pieces, axis=0).reshape(1, image_count, seq_len, model_width)
    return (
        ends,
        finals[0][None],
        finals[1][None],
        finals[2][None],
        finals[3][None],
        finals[4][None],
        finals[5][None],
    )


def solution(mesh):
    return jax.shard_map(
        shards,
        mesh=mesh,
        in_specs=(
            P("section", "dp", None, None),
            P("section", None, "dp"),
            P("section", "dp"),
            P("section", "dp", None),
            P("section", "dp", None),
            P("section", "dp", None),
            P("section", "dp", None),
        ),
        out_specs=(
            P("section", "dp", None, None),
            P("section", None, "dp"),
            P("section", "dp"),
            P("section", "dp", None),
            P("section", "dp", None),
            P("section", "dp", None),
            P("section", "dp", None),
        ),
        check_vma=False,
    )
```

profile of v0, /device:TPU:0, one launch (start us, length us, event | category | flops | bytes accessed | tf_op | source)
XLA Modules:
  0.0 814.1 jit_solution(11143844628084916837)
XLA Ops:
  9.5 43.6 %all-gather = bf16[1,8,384]{1,0,2:T(2,128)(2,1)S(1)} all-gather(bf16[1,8,24]{1,0,2:T(2,128)(2,1)S(1)} %copy.94), channel_id=2, replica_groups=mesh['section'=2,'dp'=16] {'dp'}, dimensions={2}, use_global_device_ids=true | all-gather | bytes 6528 | tf_op jit(solution)/shard_map/all_gather | solution.py:160
  53.3 11.5 %slice_reduce_fusion = (f32[384]{0:T(512)S(1)}, f32[384]{0:T(512)S(1)}, f32[384]{0:T(512)S(1)}, f32[384]{0:T(512)S(1)}, f32[384]{0:T(512)S(1)}, /*index=5*/f32[384]{0:T(512)S(1)}, f32[384]{0:T(512)S(1)}, f32[384]{0:T(512)S(1)}) fusion(f32[1,8,384]{1,0,2:T(1,128)S(1)} %convert_element_type.481), kind=kLoop, calls=%fused_computation.530 | loop fusion | flops 768 | bytes 24576 | tf_op jit(solution)/shard_map/slice | solution.py:63
  64.9 42.7 %all-gather.1 = bf16[1,384,1152]{2,1,0:T(8,128)(2,1)S(1)} all-gather(bf16[1,24,1152]{2,1,0:T(8,128)(2,1)S(1)} %copy-done.81), channel_id=3, replica_groups=mesh['section'=2,'dp'=16] {'dp'}, dimensions={1}, use_global_device_ids=true | all-gather | bytes 940032 | tf_op jit(solution)/shard_map/all_gather | solution.py:162
  111.2 38.9 %all-reduce = bf16[1536]{0:T(1024)(128)(2,1)S(1)} all-reduce(bf16[1536]{0:T(1024)(128)(2,1)S(1)} %dynamic-update-slice), channel_id=6, replica_groups=mesh['section'=2,'dp'=16] {'dp'}, use_global_device_ids=true, to_apply=%add | all-reduce | flops 1536 | bytes 6144
  150.1 37.5 %all-gather.2 = bf16[1,384,384]{2,1,0:T(8,128)(2,1)S(1)} all-gather(bf16[1,24,384]{2,1,0:T(8,128)(2,1)S(1)} %copy-done.84), channel_id=4, replica_groups=mesh['section'=2,'dp'=16] {'dp'}, dimensions={1}, use_global_device_ids=true | all-gather | bytes 313344 | tf_op jit(solution)/shard_map/all_gather | solution.py:163
  189.2 1.8 convolution_add_fusion.11
  191.1 4.5 fusion.154
  205.6 2.8 fusion.151
  208.4 2.4 collective-permute-start.1
  222.1 6.0 fusion.20
  228.2 3.9 convert_reduce_fusion.2
  237.0 1.7 copy.103
  250.3 1.5 collective-permute-start.2
  251.8 2.1 copy.107
  253.9 2.1 copy.112
  257.3 1.7 fusion.373
  261.3 2.2 convert_reduce_fusion.1
  267.6 1.7 copy.108
  277.6 2.7 convolution_add_fusion.1
  280.3 2.1 convolution_add_fusion.13
  282.4 2.8 convert_reduce_fusion
  288.0 2.1 convolution_add_fusion.12
  293.3 2.6 convolution_add_fusion
  299.4 1.9 convolution_add_fusion.4
  301.7 4.5 fusion.171
  307.4 2.1 convolution_add_fusion.2
  313.4 4.2 fusion.365
  319.1 73.7 %all-reduce.5 = (f32[8,384]{1,0:T(8,128)S(1)}, f32[1536]{0:T(1024)S(1)}) all-reduce(f32[8,384]{1,0:T(8,128)S(1)} %add_add_fusion.6, f32[1536]{0:T(1024)S(1)} %add_add_fusion.7), channel_id=8, replica_groups=mesh['section'=2,'dp'=16] {'dp'}, use_global_device_ids=true, to_apply=%region_66.67.clone | all-reduce | flops 4608 | bytes 36864
  394.0 17.2 %reduce-scatter.16.cloned.1.call-done = f32[24,384]{1,0:T(8,128)} async-done(((f32[384,384]{1,0:T(8,128)}), f32[24,384]{1,0:T(8,128)}) %reduce-scatter.16.cloned.1.call-update) | async-done | bytes 36880
  411.2 130.7 %reduce-scatter.14.cloned.1.call-done = f32[24,1152]{1,0:T(8,128)} async-done(((f32[384,1152]{1,0:T(8,128)}), f32[24,1152]{1,0:T(8,128)}) %reduce-scatter.14.cloned.1.call-update) | async-done | bytes 110608
  542.0 132.7 %reduce-scatter.10.cloned.1.call-done = f32[24,1536]{1,0:T(8,128)} async-done(((f32[384,1536]{1,0:T(8,128)}), f32[24,1536]{1,0:T(8,128)}) %reduce-scatter.10.cloned.1.call-update) | async-done | bytes 147472 | tf_op jit(solution)/shard_map/reduce_scatter | solution.py:225
  674.7 132.1 %reduce-scatter.12.cloned.1.call-done = f32[96,384]{1,0:T(8,128)} async-done(((f32[1536,384]{1,0:T(8,128)}), f32[96,384]{1,0:T(8,128)}) %reduce-scatter.12.cloned.1.call-update) | async-done | bytes 147472 | tf_op jit(solution)/shard_map/reduce_scatter | solution.py:226
  (446 shorter events, 75.2 us)
Async XLA Ops:
  7.2 57.7 %copy-start.81 = (bf16[1,24,1152]{2,1,0:T(8,128)(2,1)S(1)}, bf16[1,24,1152]{2,1,0:T(8,128)(2,1)}, u32[]{:S(2)}) copy-start(bf16[1,24,1152]{2,1,0:T(8,128)(2,1)} %param.10) | copy-start | bytes 165892
  7.2 182.1 %all-gather.9.cloned.1.call-start = ((), (), s32[]{:S(2)}) async-start(), calls=%async_computation.6 | async-start | bytes 1253376 | tf_op jit(solution)/shard_map/all_gather | solution.py:164
  7.9 183.2 %all-gather.11.cloned.1.call-start = ((), (), s32[]{:S(2)}) async-start(), calls=%async_computation.7 | async-start | bytes 1253376 | tf_op jit(solution)/shard_map/all_gather | solution.py:165
  8.7 402.6 %reduce-scatter.16.cloned.1.call-start = ((), (), s32[]{:S(2)}) async-start(), calls=%async_computation.9 | async-start | bytes 626688
  53.3 54.3 %copy-start.53 = (bf16[1,2,197,384]{3,1,2,0:T(2,128)(2,1)S(1)}, bf16[1,2,197,384]{3,1,2,0:T(2,128)(2,1)}, u32[]{:S(2)}) copy-start(bf16[1,2,197,384]{3,1,2,0:T(2,128)(2,1)} %param.7) | copy-start | bytes 907780
  64.8 140.0 %copy-start.111 = (f32[384]{0:T(512)}, f32[384]{0:T(512)S(1)}, u32[]{:S(2)}) copy-start(f32[384]{0:T(512)S(1)} %get-tuple-element.67) | copy-start | bytes 4612
  64.8 147.2 %copy-start.82 = (f32[384]{0:T(512)}, f32[384]{0:T(512)S(1)}, u32[]{:S(2)}) copy-start(f32[384]{0:T(512)S(1)} %get-tuple-element.73) | copy-start | bytes 4612
  108.0 90.1 %copy-start.30 = (bf16[1,1,197,384]{3,1,2,0:T(2,128)(2,1)}, bf16[1,1,197,384]{3,1,2,0:T(2,128)(2,1)S(1)}, u32[]{:S(2)}) copy-start(bf16[1,1,197,384]{3,1,2,0:T(2,128)(2,1)S(1)} %get-tuple-element.112) | copy-start | bytes 453892
  108.9 41.2 %copy-start.84 = (bf16[1,24,384]{2,1,0:T(8,128)(2,1)S(1)}, bf16[1,24,384]{2,1,0:T(8,128)(2,1)}, u32[]{:S(2)}) copy-start(bf16[1,24,384]{2,1,0:T(8,128)(2,1)} %param.11) | copy-start | bytes 55300
  109.4 40.7 %copy-start.41 = (bf16[197,1152]{1,0:T(8,128)(2,1)}, bf16[197,1152]{1,0:T(8,128)(2,1)S(1)}, u32[]{:S(2)}) copy-start(bf16[197,1152]{1,0:T(8,128)(2,1)S(1)} %fusion) | copy-start | bytes 1361668
  191.1 4.6 copy-start.9
  195.7 2.4 collective-permute-start
  198.2 4.8 copy-start.20
  205.6 6.8 copy-start.56
  208.4 3.3 collective-permute-start.1
  219.5 12.6 %copy-start.102 = (f32[197]{0:T(256)}, f32[197]{0:T(256)S(1)}, u32[]{:S(2)}) copy-start(f32[197]{0:T(256)S(1)} %broadcast_multiply_fusion.3) | copy-start | bytes 2368
  222.1 6.1 copy-start
  222.1 6.0 copy-start.123
  234.6 4.2 copy-start.42
  250.3 10.0 %collective-permute-start.2 = (bf16[197,384]{1,0:T(8,128)(2,1)}, bf16[197,384]{1,0:T(8,128)(2,1)}, u32[]{:S(2)}, u32[]{:S(2)}) collective-permute-start(bf16[197,384]{1,0:T(8,128)(2,1)} %get-tuple-element.131), channel_id=1, source_target_pairs={{16,0},{17,1},{18,2},{19,3},{20,4},{21,5},{22,6},{23,7},{24,8},{25... | collective-permute-start | bytes 453896 | tf_op jit(solution)/shard_map/ppermute | solution.py:17
  276.1 4.2 copy-start.35
  276.1 4.2 copy-start.50
  276.1 6.3 collective-permute-start.3
  277.5 4.9 copy-start.125
  282.4 4.4 copy-start.66
  290.0 251.9 %reduce-scatter.14.cloned.1.call-start = ((), (), s32[]{:S(2)}) async-start(), calls=%async_computation.8 | async-start | bytes 1880064
  295.9 378.8 %reduce-scatter.10.cloned.1.call-start = ((), (), s32[]{:S(2)}) async-start(), calls=%async_computation.4 | async-start | bytes 2506752 | tf_op jit(solution)/shard_map/reduce_scatter | solution.py:225
  301.3 4.8 copy-start.16
  301.3 4.8 copy-start.34
  301.3 505.4 %reduce-scatter.12.cloned.1.call-start = ((), (), s32[]{:S(2)}) async-start(), calls=%async_computation.5 | async-start | bytes 2506752 | tf_op jit(solution)/shard_map/reduce_scatter | solution.py:226
  301.6 4.5 copy-start.1
  313.4 4.3 copy-start.78
  (105 other events, 168.3 us)
Sparse Core Ops, SparseCore 0:
  10.8 59.4 all-gather.8
  73.1 56.4 all-gather.10
  290.2 121.0 reduce-scatter.15
  417.3 124.6 reduce-scatter.13
  548.0 126.5 reduce-scatter.9
  680.0 126.6 reduce-scatter.11
where the time goes:
time: 823 us; the launch traced here: 814 us
  waiting for transfers between devices  415 us (50%)
  blocking collectives  236 us (29%)
  matrix products  72 us (9%)
  other arithmetic  33 us (4%)
  local copies, waits for them, and re-layouts  31.6 us (4%)
  between operations  18.5 us (2%)
    unnamed x8, waiting for transfers between devices  149 us
    reduce_scatter x1, waiting for transfers between devices, shards(): lax.psum_scatter(totals[4], 'dp', scatter_dimension=0, tiled=True)  133 us
    reduce_scatter x1, waiting for transfers between devices, shards(): lax.psum_scatter(totals[5], 'dp', scatter_dimension=0, tiled=True)  132 us
    unnamed x2, blocking collectives  113 us
    all_gather x1, blocking collectives, shards(): lax.all_gather(vectors[0], 'dp', axis=1, tiled=True)  43.6 us
    all_gather x1, blocking collectives, shards(): lax.all_gather(w_qkv[0], 'dp', axis=0, tiled=True)  42.7 us
    all_gather x1, blocking collectives, shards(): lax.all_gather(w_out[0], 'dp', axis=0, tiled=True)  37.5 us
    unnamed x259, local copies, waits for them, and re-layouts  16.7 us
  transfers between devices with their start and end apart: 10, of which 6 were waited for; matrix products, arithmetic and copies ran while one was open for 7% of the time, Pallas kernels for 0%

commit v1 on v0

v1 whole, which is shorter than its diff:
```python
import functools

import jax
import jax.numpy as jnp
from jax import lax
from jax.experimental import pallas as pl
from jax.experimental.pallas import tpu as pltpu
from jax.sharding import PartitionSpec as P

HEADS = 6
HEAD_DIM = 64
PAIR = 2 * HEAD_DIM
EPS = 1e-06
SCALE = HEAD_DIM ** (-0.5)
VMEM_BYTES = 56 * 1024 * 1024

bf16 = jnp.bfloat16
f32 = jnp.float32
MESH = pl.DeviceIdType.MESH


def chip_grid(count):
    for side in range(1, count + 1):
        if 2 * side**3 == count:
            return (2 * side, side, side)
    return (count, 1, 1)


def place(dims):
    me = lax.axis_index("dp")
    _, size_y, size_x = dims
    return me // (size_y * size_x), (me // size_x) % size_y, me % size_x


def rank(dims, z, y, x):
    return (z * dims[1] + y) * dims[2] + x


def greet(dims, s, z, y, x):
    barrier = pltpu.get_barrier_semaphore()
    count = 1
    pl.semaphore_signal(barrier, inc=1, device_id={"section": 1 - s}, device_id_type=MESH)
    for axis, (size, at) in enumerate(zip(dims, (z, y, x))):
        for d in range(1, size):
            there = [z, y, x]
            there[axis] = (at + d) % size
            pl.semaphore_signal(barrier, inc=1, device_id={"dp": rank(dims, *there)}, device_id_type=MESH)
            count += 1
    pl.semaphore_wait(barrier, count)


def gather_kernel(dims, rows_a, shard_ref, img_ref, out_ref, img_out, own_sem, img_sems, send_sems, recv_sems, core_send, core_recv):
    size_z, size_y, size_x = dims
    s = lax.axis_index("section")
    z, y, x = place(dims)
    rows = shard_ref.shape[0]
    part_a, part_b = pl.ds(0, rows_a), pl.ds(rows_a, rows - rows_a)
    greet(dims, s, z, y, x)
    mine = out_ref.at[s]
    waiting = []
    counter = [0, 0]

    def remote(src, dst, there):
        slot = counter[0]
        counter[0] += 1
        copy = pltpu.make_async_remote_copy(
            src_ref=src, dst_ref=dst, send_sem=send_sems.at[slot], recv_sem=recv_sems.at[slot],
            device_id={"dp": rank(dims, *there)}, device_id_type=MESH,
        )
        copy.start()
        waiting.append(copy)
        return copy

    arriving = []

    def to_core(piece, other):
        slot = counter[1]
        counter[1] += 1
        copy = pltpu.make_async_remote_copy(
            src_ref=piece, dst_ref=piece, send_sem=core_send.at[slot], recv_sem=core_recv.at[slot],
            device_id={"section": 1 - s}, device_id_type=MESH,
        )
        copy.start()
        waiting.append(copy)
        arriving.append(pltpu.make_async_remote_copy(
            src_ref=other, dst_ref=other, send_sem=core_send.at[slot], recv_sem=core_recv.at[slot],
            device_id={"section": 1 - s}, device_id_type=MESH,
        ))

    def block(section, at_z, at_y, at_x, part):
        return out_ref.at[section, at_z, at_y, at_x, part]

    image = pltpu.make_async_remote_copy(
        src_ref=img_ref.at[1 - s], dst_ref=img_out, send_sem=img_sems.at[0], recv_sem=img_sems.at[1],
        device_id={"section": 1 - s}, device_id_type=MESH,
    )
    image.start()
    every = slice(None)
    whole = pl.ds(0, rows)
    first = [
        (remote(shard_ref, mine.at[z, y, x], ((z + d) % size_z, y, x)), (z - d + size_z) % size_z)
        for d in range(1, size_z)
    ]
    own = pltpu.make_async_copy(shard_ref, mine.at[z, y, x], own_sem)
    own.start()
    own.wait()
    to_core(block(s, z, y, x, whole), block(1 - s, z, y, x, whole))
    for copy, from_z in first:
        copy.wait_recv()
        to_core(block(s, from_z, y, x, whole), block(1 - s, from_z, y, x, whole))

    second = []
    for d in range(1, size_y):
        piece = block(s, every, y, x, part_a)
        second.append((remote(piece, piece, (z, (y + d) % size_y, x)), 0, (y - d + size_y) % size_y))
    for d in range(1, size_x):
        piece = block(s, every, y, x, part_b)
        second.append((remote(piece, piece, (z, y, (x + d) % size_x)), 1, (x - d + size_x) % size_x))
    for copy, kind, at in second:
        copy.wait_recv()
        if kind == 0:
            to_core(block(s, every, at, x, part_a), block(1 - s, every, at, x, part_a))
        else:
            to_core(block(s, every, y, at, part_b), block(1 - s, every, y, at, part_b))

    third = []
    for d in range(1, size_x):
        piece = block(s, every, every, x, part_a)
        third.append((remote(piece, piece, (z, y, (x + d) % size_x)), 0, (x - d + size_x) % size_x))
    for d in range(1, size_y):
        piece = block(s, every, y, every, part_b)
        third.append((remote(piece, piece, (z, (y + d) % size_y, x)), 1, (y - d + size_y) % size_y))
    for copy, kind, at in third:
        copy.wait_recv()
        if kind == 0:
            to_core(block(s, every, every, at, part_a), block(1 - s, every, every, at, part_a))
        else:
            to_core(block(s, every, at, every, part_b), block(1 - s, every, at, every, part_b))
    for copy in waiting:
        copy.wait_send()
    for copy in arriving:
        copy.wait_recv()
    image.wait()


def gather(dims, shard, images):
    rows, width = shard.shape
    rows_a = 16 * (rows // 32)
    size_z, size_y, size_x = dims
    across = (size_z - 1) + 2 * (size_y - 1) + 2 * (size_x - 1)
    any_spec = pl.BlockSpec(memory_space=pl.ANY)
    return pl.pallas_call(
        functools.partial(gather_kernel, dims, rows_a),
        out_shape=(
            jax.ShapeDtypeStruct((2,) + dims + (rows, width), bf16),
            jax.ShapeDtypeStruct(images.shape[1:], bf16),
        ),
        in_specs=[any_spec] * 2,
        out_specs=(any_spec, any_spec),
        scratch_shapes=[
            pltpu.SemaphoreType.DMA,
            pltpu.SemaphoreType.DMA((2,)),
            pltpu.SemaphoreType.DMA((max(across, 1),)),
            pltpu.SemaphoreType.DMA((max(across, 1),)),
            pltpu.SemaphoreType.DMA((across + 1,)),
            pltpu.SemaphoreType.DMA((across + 1,)),
        ],
        compiler_params=pltpu.CompilerParams(collective_id=0, has_side_effects=True, vmem_limit_bytes=VMEM_BYTES),
        name="weight_gather",
    )(shard, images)


def scatter_kernel(dims, rows_a, part_ref, rows_ref, out_ref, rows_out, core_in, work, in_one_a, in_one_b,
                   two_a, two_b, in_two_a, in_two_b, three, in_three, row_sems, send_sems, recv_sems, core_send, core_recv):
    size_z, size_y, size_x = dims
    s = lax.axis_index("section")
    z, y, x = place(dims)
    rows = out_ref.shape[0]
    part_a, part_b = pl.ds(0, rows_a), pl.ds(rows_a, rows - rows_a)
    every = slice(None)
    greet(dims, s, z, y, x)
    waiting = []
    counter = [0]

    def remote(src, dst, there):
        slot = counter[0]
        counter[0] += 1
        copy = pltpu.make_async_remote_copy(
            src_ref=src, dst_ref=dst, send_sem=send_sems.at[slot], recv_sem=recv_sems.at[slot],
            device_id={"dp": rank(dims, *there)}, device_id_type=MESH,
        )
        copy.start()
        waiting.append(copy)
        return copy

    chunks = []
    for d in list(range(1, max(size_x, size_y))) + [0]:
        if d < size_x:
            chunks.append((0, d, (x + d) % size_x))
        if d < size_y:
            chunks.append((1, d, (y + d) % size_y))
    cores = []
    for slot, (kind, d, at) in enumerate(chunks):
        if kind == 0:
            src, dst = part_ref.at[1 - s, :, :, at, part_a], core_in.at[:, :, at, part_a]
        else:
            src, dst = part_ref.at[1 - s, :, at, :, part_b], core_in.at[:, at, :, part_b]
        copy = pltpu.make_async_remote_copy(
            src_ref=src, dst_ref=dst, send_sem=core_send.at[slot], recv_sem=core_recv.at[slot],
            device_id={"section": 1 - s}, device_id_type=MESH,
        )
        copy.start()
        cores.append(copy)
    row_copy = pltpu.make_async_remote_copy(
        src_ref=rows_ref.at[s], dst_ref=rows_out, send_sem=row_sems.at[0], recv_sem=row_sems.at[1],
        device_id={"section": 1 - s}, device_id_type=MESH,
    )
    row_copy.start()

    one_a, one_b = [], []
    for copy, (kind, d, at) in zip(cores, chunks):
        copy.wait_recv()
        if kind == 0:
            @pl.loop(0, size_z * size_y)
            def _(i):
                u, v = i // size_y, i % size_y
                work[u, v, at, part_a] = (
                    part_ref[s, u, v, at, part_a].astype(f32) + core_in[u, v, at, part_a].astype(f32)
                ).astype(bf16)
            if d:
                one_a.append(remote(work.at[:, :, at, part_a], in_one_a.at[d - 1], (z, y, at)))
        else:
            @pl.loop(0, size_z * size_x)
            def _(i):
                u, v = i // size_x, i % size_x
                work[u, at, v, part_b] = (
                    part_ref[s, u, at, v, part_b].astype(f32) + core_in[u, at, v, part_b].astype(f32)
                ).astype(bf16)
            if d:
                one_b.append(remote(work.at[:, at, :, part_b], in_one_b.at[d - 1], (z, at, x)))

    for copy in one_a:
        copy.wait_recv()

    @pl.loop(0, size_z * size_y)
    def _(i):
        u, v = i // size_y, i % size_y
        total = work[u, v, x, part_a].astype(f32)
        for d in range(1, size_x):
            total = total + in_one_a[d - 1, u, v].astype(f32)
        two_a[v, u] = total.astype(bf16)

    go_a = [remote(two_a.at[(y + d) % size_y], in_two_a.at[d - 1], (z, (y + d) % size_y, x)) for d in range(1, size_y)]
    for copy in one_b:
        copy.wait_recv()

    @pl.loop(0, size_z * size_x)
    def _(i):
        u, v = i // size_x, i % size_x
        total = work[u, y, v, part_b].astype(f32)
        for d in range(1, size_y):
            total = total + in_one_b[d - 1, u, v].astype(f32)
        two_b[v, u] = total.astype(bf16)

    go_b = [remote(two_b.at[(x + d) % size_x], in_two_b.at[d - 1], (z, y, (x + d) % size_x)) for d in range(1, size_x)]
    for copy in go_a + go_b:
        copy.wait_recv()

    @pl.loop(0, size_z)
    def _(u):
        total = two_a[y, u].astype(f32)
        for d in range(1, size_y):
            total = total + in_two_a[d - 1, u].astype(f32)
        three[u, part_a] = total.astype(bf16)
        total = two_b[x, u].astype(f32)
        for d in range(1, size_x):
            total = total + in_two_b[d - 1, u].astype(f32)
        three[u, part_b] = total.astype(bf16)

    last = [remote(three.at[(z + d) % size_z], in_three.at[d - 1], ((z + d) % size_z, y, x)) for d in range(1, size_z)]
    for copy in last:
        copy.wait_recv()
    total = three[z].astype(f32)
    for d in range(1, size_z):
        total = total + in_three[d - 1].astype(f32)
    out_ref[...] = total
    for copy in waiting + cores:
        copy.wait_send()
    row_copy.wait()


def scatter(dims, partials, rows_pair):
    rows, width = partials.shape[-2:]
    rows_a = 16 * (rows // 32)
    rows_b = rows - rows_a
    size_z, size_y, size_x = dims
    across = (size_z - 1) + 2 * (size_y - 1) + 2 * (size_x - 1)
    vmem = pl.BlockSpec(memory_space=pltpu.VMEM)
    any_spec = pl.BlockSpec(memory_space=pl.ANY)
    more = lambda size: max(size - 1, 1)
    return pl.pallas_call(
        functools.partial(scatter_kernel, dims, rows_a),
        out_shape=(
            jax.ShapeDtypeStruct((rows, width), f32),
            jax.ShapeDtypeStruct(rows_pair.shape[1:], bf16),
        ),
        in_specs=[vmem, any_spec],
        out_specs=(vmem, any_spec),
        scratch_shapes=[
            pltpu.VMEM(dims + (rows, width), bf16),
            pltpu.VMEM(dims + (rows, width), bf16),
            pltpu.VMEM((more(size_x), size_z, size_y, rows_a, width), bf16),
            pltpu.VMEM((more(size_y), size_z, size_x, rows_b, width), bf16),
            pltpu.VMEM((size_y, size_z, rows_a, width), bf16),
            pltpu.VMEM((size_x, size_z, rows_b, width), bf16),
            pltpu.VMEM((more(size_y), size_z, rows_a, width), bf16),
            pltpu.VMEM((more(size_x), size_z, rows_b, width), bf16),
            pltpu.VMEM((size_z, rows, width), bf16),
            pltpu.VMEM((more(size_z), rows, width), bf16),
            pltpu.SemaphoreType.DMA((2,)),
            pltpu.SemaphoreType.DMA((max(across, 1),)),
            pltpu.SemaphoreType.DMA((max(across, 1),)),
            pltpu.SemaphoreType.DMA((size_x + size_y,)),
            pltpu.SemaphoreType.DMA((size_x + size_y,)),
        ],
        compiler_params=pltpu.CompilerParams(collective_id=1, has_side_effects=True, vmem_limit_bytes=VMEM_BYTES),
        name="grad_scatter",
    )(partials, rows_pair)


def mm(left, right):
    return jnp.dot(left, right, preferred_element_type=f32)


def mm_t(left, right):
    return lax.dot_general(left, right, (((1,), (1,)), ((), ())), preferred_element_type=f32)


def t_mm(left, right):
    return lax.dot_general(left, right, (((0,), (0,)), ((), ())), preferred_element_type=f32)


def norm_parts(values):
    average = jnp.mean(values, axis=-1, keepdims=True)
    centered = values - average
    inverse = lax.rsqrt(jnp.mean(centered * centered, axis=-1, keepdims=True) + EPS)
    return centered * inverse, inverse


def norm_back(unit, inverse, gain, grad):
    scaled = grad * (1.0 + gain)
    mean_one = jnp.mean(scaled, axis=-1, keepdims=True)
    mean_two = jnp.mean(scaled * unit, axis=-1, keepdims=True)
    return (
        inverse * (scaled - mean_one - unit * mean_two),
        jnp.sum(grad * unit, axis=0, keepdims=True),
        jnp.sum(grad, axis=0, keepdims=True),
    )


def layers_kernel(seq, rows_ref, cot_ref, vec_ref, bias_ref, qkv_ref, wo_ref, up_ref, down_ref,
                  y_ref, dh_ref, gvec_ref, gbias_ref, gqkv_ref, gwo_ref, gup_ref, gdown_ref,
                  h_s, a_s, q_s, o_s, z_s, n_s, g_s, slope_s, pf_s, dn_s, dy_s, dqkv_s):
    rows, width = cot_ref.shape
    ff = up_ref.shape[-1]
    pairs = width // PAIR
    lane = lax.broadcasted_iota(jnp.int32, (rows, PAIR), 1)
    low_half = lane < HEAD_DIM
    key_ok = lax.broadcasted_iota(jnp.int32, (rows, rows), 1) < seq
    zero = jnp.zeros((rows, PAIR), bf16)

    def halves(values):
        return jnp.where(low_half, values, zero), jnp.where(low_half, zero, values)

    h_s[0] = rows_ref[...].astype(f32)

    @pl.loop(0, 2)
    def _(e):
        vec = vec_ref[e]
        h = h_s[e]
        unit, _ = norm_parts(h)
        a = (unit * (1.0 + vec[0:1]) + vec[1:2]).astype(bf16)
        a_s[e] = a
        for third in range(3):
            cols = slice(third * width, (third + 1) * width)
            part = mm(a, qkv_ref[e, :, cols])
            if third != 1:
                part = part + vec[2 + third // 2:3 + third // 2]
            q_s[e, :, cols] = part.astype(bf16)
        for j in range(pairs):
            q = q_s[e, :, j * PAIR:(j + 1) * PAIR]
            k = q_s[e, :, width + j * PAIR:width + (j + 1) * PAIR]
            v = q_s[e, :, 2 * width + j * PAIR:2 * width + (j + 1) * PAIR]
            outs = []
            for i, q_half in enumerate(halves(q)):
                scores = jnp.where(key_ok, mm_t(q_half, k) * SCALE, -1e30)
                shifted = jnp.exp(scores - jnp.max(scores, axis=-1, keepdims=True))
                pf = shifted / jnp.sum(shifted, axis=-1, keepdims=True)
                pf_s[e, 2 * j + i] = pf
                outs.append(mm(pf.astype(bf16), v))
            o_s[e, :, j * PAIR:(j + 1) * PAIR] = jnp.where(low_half, outs[0], outs[1]).astype(bf16)
        z = h + mm(o_s[e], wo_ref[e]) + vec[4:5]
        z_s[e] = z
        unit, _ = norm_parts(z)
        n = (unit * (1.0 + vec[5:6]) + vec[6:7]).astype(bf16)
        n_s[e] = n
        for c in range(ff // width):
            cols = slice(c * width, (c + 1) * width)
            u = mm(n, up_ref[e, :, cols]) + bias_ref[e, :, cols]
            phi = 0.5 + 0.5 * lax.erf(u * (0.5 ** 0.5))
            g_s[e, :, cols] = (u * phi).astype(bf16)
            slope_s[e, :, cols] = phi + u * (jnp.exp(-0.5 * u * u) * 0.3989422804014327)
        result = (z + mm(g_s[e], down_ref[e]) + vec[7:8]).astype(bf16)
        y_ref[...] = result
        h_s[1] = jnp.where(e == 0, result.astype(f32), h_s[1])

    dy_s[...] = cot_ref[...].astype(f32)

    @pl.loop(0, 2)
    def _(step):
        e = 1 - step
        vec = vec_ref[e]
        dy = dy_s[...]
        dm = dy.astype(bf16)
        g7 = jnp.sum(dm.astype(f32), axis=0, keepdims=True)
        n = n_s[e]
        for c in range(ff // width):
            cols = slice(c * width, (c + 1) * width)
            gdown_ref[e, cols, :] = t_mm(g_s[e, :, cols], dm).astype(bf16)
            du = (mm_t(dm, down_ref[e, cols, :]) * slope_s[e, :, cols]).astype(bf16)
            gbias_ref[e, :, cols] = jnp.sum(du.astype(f32), axis=0, keepdims=True)
            gup_ref[e, :, cols] = t_mm(n, du).astype(bf16)
            back = mm_t(du, up_ref[e, :, cols])
            if c == 0:
                dn_s[...] = back
            else:
                dn_s[...] += back
        unit, inverse = norm_parts(z_s[e])
        dz, g5, g6 = norm_back(unit, inverse, vec[5:6], dn_s[...])
        dz = dz + dy
        dr = dz.astype(bf16)
        g4 = jnp.sum(dr.astype(f32), axis=0, keepdims=True)
        gwo_ref[e] = t_mm(o_s[e], dr).astype(bf16)
        do_all = mm_t(dr, wo_ref[e]).astype(bf16)
        for j in range(pairs):
            q = q_s[e, :, j * PAIR:(j + 1) * PAIR]
            k = q_s[e, :, width + j * PAIR:width + (j + 1) * PAIR]
            v = q_s[e, :, 2 * width + j * PAIR:2 * width + (j + 1) * PAIR]
            do = do_all[:, j * PAIR:(j + 1) * PAIR]
            dq, dk, dv = [], [], []
            for i, do_half in enumerate(halves(do)):
                pf = pf_s[e, 2 * j + i]
                dp = mm_t(do_half, v)
                ds = (pf * (dp - jnp.sum(pf * dp, axis=-1, keepdims=True))).astype(bf16)
                dv.append(t_mm(pf.astype(bf16), do))
                dq.append(mm(ds, k))
                dk.append(t_mm(ds, q))
            dqkv_s[:, j * PAIR:(j + 1) * PAIR] = (jnp.where(low_half, dq[0], dq[1]) * SCALE).astype(bf16)
            dqkv_s[:, width + j * PAIR:width + (j + 1) * PAIR] = (jnp.where(low_half, dk[0], dk[1]) * SCALE).astype(bf16)
            dqkv_s[:, 2 * width + j * PAIR:2 * width + (j + 1) * PAIR] = jnp.where(low_half, dv[0], dv[1]).astype(bf16)
        a = a_s[e]
        sums = []
        for third in range(3):
            cols = slice(third * width, (third + 1) * width)
            dpart = dqkv_s[:, cols]
            sums.append(jnp.sum(dpart.astype(f32), axis=0, keepdims=True))
            gqkv_ref[e, :, cols] = t_mm(a, dpart).astype(bf16)
            back = mm_t(dpart, qkv_ref[e, :, cols])
            if third == 0:
                dn_s[...] = back
            else:
                dn_s[...] += back
        unit, inverse = norm_parts(h_s[e])
        dh, g0, g1 = norm_back(unit, inverse, vec[0:1], dn_s[...])
        low = (dz + dh).astype(bf16)
        dh_ref[...] = low
        dy_s[...] = low.astype(f32)
        for row, value in enumerate((g0, g1, sums[0], sums[2], g4, g5, g6, g7)):
            gvec_ref[e, row:row + 1, :] = value


def run_layers(seq, rows, cot, vec, bias, qkv, wo, up, down):
    t, width = rows.shape
    ff = up.shape[-1]
    vmem = pl.BlockSpec(memory_space=pltpu.VMEM)
    shape = jax.ShapeDtypeStruct
    return pl.pallas_call(
        functools.partial(layers_kernel, seq),
        out_shape=(
            shape((t, width), bf16), shape((t, width), bf16), shape(vec.shape, f32), shape(bias.shape, f32),
            shape(qkv.shape, bf16), shape(wo.shape, bf16), shape(up.shape, bf16), shape(down.shape, bf16),
        ),
        in_specs=[vmem] * 8,
        out_specs=(vmem,) * 8,
        scratch_shapes=[
            pltpu.VMEM((2, t, width), f32),
            pltpu.VMEM((2, t, width), bf16),
            pltpu.VMEM((2, t, 3 * width), bf16),
            pltpu.VMEM((2, t, width), bf16),
            pltpu.VMEM((2, t, width), f32),
            pltpu.VMEM((2, t, width), bf16),
            pltpu.VMEM((2, t, ff), bf16),
            pltpu.VMEM((2, t, ff), f32),
            pltpu.VMEM((2, HEADS, t, t), f32),
            pltpu.VMEM((t, width), f32),
            pltpu.VMEM((t, width), f32),
            pltpu.VMEM((t, 3 * width), bf16),
        ],
        compiler_params=pltpu.CompilerParams(vmem_limit_bytes=VMEM_BYTES),
        name="two_layers",
    )(rows, cot, vec, bias, qkv, wo, up, down)


def split_cols(matrix, count, width):
    lead, (tall, wide) = matrix.shape[:-2], matrix.shape[-2:]
    per, across = tall // count, wide // width
    blocks = jnp.swapaxes(matrix.reshape(lead + (count, per, across, width)), -3, -2)
    return blocks.reshape(lead + (count, across * per, width))


def join_cols(blocks, per, width):
    lead, (count, tall) = blocks.shape[:-3], blocks.shape[-3:-1]
    across = tall // per
    matrix = jnp.swapaxes(blocks.reshape(lead + (count, across, per, width)), -3, -2)
    return matrix.reshape(lead + (count * per, across * width))


def pack(count, width, small, qkv, wo, up, down):
    lead = small.shape[:-2]
    pieces = [split_cols(m, count, width) for m in (qkv, wo, up, down)]
    used = sum(piece.shape[-2] for piece in pieces)
    small_rows = -(-small.shape[-1] // width)
    rows = -(-(used + small_rows) // 16) * 16
    room = (rows - used) * width
    padded = jnp.pad(small, [(0, 0)] * (small.ndim - 1) + [(0, room - small.shape[-1])])
    pieces.append(padded.reshape(lead + (count, rows - used, width)))
    return jnp.concatenate(pieces, axis=-2)


def unpack(blocks, per, ff_per, ff, vec_rows):
    width = blocks.shape[-1]
    ends = [3 * per, 4 * per, 4 * per + (ff // width) * per]
    ends.append(ends[-1] + ff_per)
    qkv = join_cols(blocks[..., :ends[0], :], per, width)
    wo = join_cols(blocks[..., ends[0]:ends[1], :], per, width)
    up = join_cols(blocks[..., ends[1]:ends[2], :], per, width)
    down = join_cols(blocks[..., ends[2]:ends[3], :], ff_per, width)
    tail = blocks[..., ends[3]:, :]
    small = tail.reshape(tail.shape[:-2] + (-1,))
    vec = small[..., :vec_rows * per].reshape(small.shape[:-1] + (vec_rows, per))
    vec = jnp.moveaxis(vec, -2, -3)
    vec = vec.reshape(vec.shape[:-2] + (-1,))
    bias = small[..., vec_rows * per:vec_rows * per + ff_per]
    bias = bias.reshape(bias.shape[:-2] + (-1,))
    return vec, bias, qkv, wo, up, down


def shards(dims, ends_in, vectors, up_bias, w_qkv, w_out, w_up, w_down):
    section_id = lax.axis_index("section")
    is_first = section_id == 0
    local = ends_in[0]
    _, seq, width = local.shape
    count = dims[0] * dims[1] * dims[2]
    vec_rows, per = vectors.shape[1:]
    ff_per = up_bias.shape[1]
    ff = ff_per * count
    t = -(-seq // 16) * 16
    padded = jnp.pad(local, ((0, 0), (0, t - seq), (0, 0)))
    small = jnp.concatenate([vectors[0].reshape(1, -1), up_bias], axis=-1)
    shard = pack(1, width, small, w_qkv[0], w_out[0], w_up[0], w_down[0])[0]
    blocks, other = gather(dims, shard, padded)
    vec, bias, qkv, wo, up, down = unpack(blocks.reshape((2, count) + shard.shape), per, ff_per, ff, vec_rows)
    own = lax.dynamic_index_in_dim(padded, section_id, 0, keepdims=False)
    rows = jnp.where(is_first, own, other)
    cot = jnp.where(is_first, other, own)
    y, dh, gvec, gbias, gqkv, gwo, gup, gdown = run_layers(
        seq, rows, cot, vec.astype(f32), bias.astype(f32)[:, None], qkv, wo, up, down
    )
    gvec = jnp.moveaxis(gvec.reshape(2, vec_rows, count, per), 2, 1).reshape(2, count, vec_rows * per)
    gsmall = jnp.concatenate([gvec, gbias.reshape(2, count, ff_per)], axis=-1).astype(bf16)
    partials = pack(count, width, gsmall, gqkv, gwo, gup, gdown)
    total, got = scatter(dims, partials.reshape((2,) + dims + partials.shape[-2:]), jnp.stack([y, dh]))
    fvec, fbias, fqkv, fwo, fup, fdown = unpack(total[None], per, ff_per, ff, vec_rows)
    ends = jnp.stack([jnp.where(is_first, dh, got), jnp.where(is_first, got, y)])[None, :, :seq]
    return ends, fvec[None], fbias[None], fqkv[None], fwo[None], fup[None], fdown[None]


def solution(mesh):
    dims = chip_grid(mesh.shape["dp"])
    specs = (
        P("section", "dp", None, None),
        P("section", None, "dp"),
        P("section", "dp"),
        P("section", "dp", None),
        P("section", "dp", None),
        P("section", "dp", None),
        P("section", "dp", None),
    )
    return jax.shard_map(
        functools.partial(shards, dims), mesh=mesh, in_specs=specs, out_specs=specs, check_vma=False
    )
```

time: 823 us -> 206 us (0.25)
  waiting for transfers between devices: 415 us -> 0 us
  blocking collectives: 236 us -> 0 us
  Pallas kernels: 0 us -> 149 us
  matrix products: 72 us -> 0 us
  other arithmetic: 33 us -> 4.41 us
  between operations: 18.5 us -> 0.85 us
  local copies, waits for them, and re-layouts: 31.6 us -> 49 us
    reduce_scatter x2 -> x0, waiting for transfers between devices: 265 us -> none  [the longest x1 133 us: shards(): lax.psum_scatter(totals[4], 'dp', scatter_dimension=0, tiled=True)]
    unnamed x8 -> x0, waiting for transfers between devices: 149 us -> none
    pallas_call x0 -> x3, Pallas kernels: none -> 149 us  [the longest x1 67.1 us: scatter(): pl.pallas_call(functools.partial(scatter_kernel, dims, rows_a), out_shape...]
    all_gather x3 -> x0, blocking collectives: 124 us -> none  [the longest x1 43.6 us: shards(): lax.all_gather(vectors[0], 'dp', axis=1, tiled=True)]
    unnamed x2 -> x0, blocking collectives: 113 us -> none
    dot_general x57 -> x0, matrix products: 72 us -> none  [the longest x3 11.6 us: forward_layer(): jnp.dot(activated, down_all, preferred_element_type=jnp.float32)]
    reshape x13 -> x12, local copies, waits for them, and re-layouts: 0.1 us -> 14.9 us  [the longest x3 7.96 us: split_cols(): matrix.reshape(lead + (count, per, across, width))]
    slice x4 -> x9, local copies, waits for them, and re-layouts: 0.43 us -> 13.6 us  [the longest x2 6.04 us: unpack(): down = join_cols(blocks[..., ends[2]:ends[3], :], ff_per, width)]
  transfers between devices with their start and end apart: 10 -> 0, of which waited for: 6 -> 0; matrix products, arithmetic and copies ran while one was open for 7% -> 0% of each run, Pallas kernels for 0% -> 0%
where the time goes in v1:
time: 206 us; the launch traced here: 204 us
  Pallas kernels  149 us (72%)
  local copies, waits for them, and re-layouts  49 us (24%)
  other arithmetic  4.41 us (2%)
    pallas_call x1, Pallas kernels, scatter(): pl.pallas_call(functools.partial(scatter_kernel, dims, rows_a), out_shape...  67.1 us
    pallas_call x1, Pallas kernels, gather(): pl.pallas_call(functools.partial(gather_kernel, dims, rows_a), out_shape=...  59.4 us
    pallas_call x1, Pallas kernels, run_layers(): pl.pallas_call(functools.partial(layers_kernel, seq), out_shape=(shape((t...  22.8 us
    unnamed x27, local copies, waits for them, and re-layouts  11.6 us
    reshape x3, local copies, waits for them, and re-layouts, split_cols(): matrix.reshape(lead + (count, per, across, width))  7.96 us
    slice x2, local copies, waits for them, and re-layouts, unpack(): down = join_cols(blocks[..., ends[2]:ends[3], :], ff_per, width)  6.04 us
    reshape x2, local copies, waits for them, and re-layouts, join_cols(): return matrix.reshape(lead + (count * per, across * width))  5.53 us

profile of v1, /device:TPU:0, one launch (start us, length us, event | category | flops | bytes accessed | tf_op | source)
XLA Modules:
  0.0 203.5 jit_solution(10698066337240316613)
XLA Ops:
  0.6 1.0 copy.59
  1.6 0.8 pad.12.img_ref
  2.4 0.8 reshape_squeeze.9
  4.0 0.9 copy.62
  4.9 0.9 constant_dynamic-update-slice_fusion.1
  5.8 0.8 reshape_squeeze.11
  6.6 0.8 fusion.5
  8.1 59.4 %weight_gather.1 = (bf16[2,4,2,2,304,384]{5,4,3,2,1,0:T(8,128)(2,1)}, bf16[208,384]{1,0:T(8,128)(2,1)}) custom-call(bf16[304,384]{1,0:T(8,128)(2,1)} %bitcast.96, bf16[2,208,384]{2,1,0:T(8,128)(2,1)} %pad.12.img_ref), custom_call_target="tpu_custom_call" | custom-call | tf_op jit(solution)/shard_map/weight_gather/pallas_call | solution.py:152
  67.5 1.7 bitcast_select_fusion
  69.1 4.4 %fusion.6 = (bf16[2,16,96,384]{3,2,1,0:T(8,128)(2,1)}, bf16[2,16,96,384]{3,2,1,0:T(8,128)(2,1)S(1)}) fusion(bf16[2,16,304,384]{3,2,1,0:T(8,128)(2,1)} %bitcast.73), kind=kLoop, calls=%fused_computation.35 | loop fusion | bytes 9437184 | tf_op jit(solution)/shard_map/slice | solution.py:547
  73.5 0.9 copy.58
  74.4 2.3 %reshape.109.up_ref = bf16[2,384,1536]{2,1,0:T(8,128)(2,1)} reshape(bf16[2,16,24,4,384]{4,3,2,1,0:T(4,128)(2,1)S(1)} %bitcast.69) | data formatting | bytes 4718592 | tf_op jit(solution)/shard_map/reshape | solution.py:525
  76.8 1.0 slice.60
  79.7 1.7 slice.63
  81.3 0.9 copy.41
  82.2 3.2 %reshape.107.qkv_ref = bf16[2,384,1152]{2,1,0:T(8,128)(2,1)} reshape(bf16[2,16,24,3,384]{4,3,2,1,0:T(4,128)(2,1)S(1)} %copy.41) | data formatting | bytes 3538944 | tf_op jit(solution)/shard_map/reshape | solution.py:525
  85.4 1.9 slice.64
  87.3 22.8 %two_layers.1 = (bf16[208,384]{1,0:T(8,128)(2,1)}, bf16[208,384]{1,0:T(8,128)(2,1)}, f32[2,8,384]{2,1,0:T(8,128)}, f32[2,1,1536]{2,1,0:T(1,128)}, bf16[2,384,115...) custom-call(bf16[208,384]{1,0:T(8,128)(2,1)} %get-tuple-element.57.r, ...), custom_call_target="tpu_custom_call" | custom-call | tf_op jit(solution)/shard_map/two_layers/pallas_call | solution.py:487
  110.2 3.3 %reshape.110 = bf16[2,16,24,3,384]{4,3,2,1,0:T(4,128)(2,1)S(1)} reshape(bf16[2,384,1152]{2,1,0:T(8,128)(2,1)} %get-tuple-element.22) | data formatting | bytes 3538944 | tf_op jit(solution)/shard_map/reshape | solution.py:517
  113.8 1.4 constant_dynamic-update-slice_fusion.9
  115.1 0.9 constant_dynamic-update-slice_fusion.8
  116.1 4.3 %reshape.111 = bf16[2,16,24,4,384]{4,3,2,1,0:T(4,128)(2,1)S(1)} reshape(bf16[2,384,1536]{2,1,0:T(8,128)(2,1)} %get-tuple-element.24) | data formatting | bytes 4718592 | tf_op jit(solution)/shard_map/reshape | solution.py:517
  120.7 1.7 constant_dynamic-update-slice_fusion.7
  122.4 0.8 copy-done
  123.3 1.7 constant_dynamic-update-slice_fusion.6
  125.5 0.8 constant_dynamic-update-slice_fusion.5.part_ref
  127.0 67.1 %grad_scatter.1 = (f32[304,384]{1,0:T(8,128)}, bf16[208,384]{1,0:T(8,128)(2,1)}) custom-call(bf16[2,4,2,2,304,384]{5,4,3,2,1,0:T(8,128)(2,1)} %constant_dynamic-update-slice_fusion.5.part_ref, bf16[2,208,384]{2,1,0:T(8,128)(2,1)} %pad_maximum_fusion.rows_ref), custom_call_target="tpu_custom_call" | custom-call | tf_op jit(solution)/shard_map/grad_scatter/pallas_call | solution.py:301
  194.2 1.0 select_bitcast_fusion.1
  195.2 1.0 copy.48
  196.1 1.7 fusion.7
  198.4 0.9 slice.70
  202.2 1.4 slice.71
  (46 shorter events, 8.6 us)
Async XLA Ops:
  7.4 0.7 copy-start.4
  113.7 1.4 copy-start.3
  120.7 2.5 %copy-start = (bf16[2,1536,384]{2,1,0:T(8,128)(2,1)S(1)}, bf16[2,1536,384]{2,1,0:T(8,128)(2,1)}, u32[]{:S(2)}) copy-start(bf16[2,1536,384]{2,1,0:T(8,128)(2,1)} %get-tuple-element.25) | copy-start | bytes 7077892
  123.3 1.7 copy-start.5
  123.3 1.9 copy-start.6
  124.9 1.4 copy-start.1
  124.9 1.4 copy-start.2

commit v2 on v1

v2 whole, which is shorter than its diff:
```python
import functools

import jax
import jax.numpy as jnp
from jax import lax
from jax.experimental import pallas as pl
from jax.experimental.pallas import tpu as pltpu
from jax.sharding import PartitionSpec as P

HEADS = 6
HEAD_DIM = 64
PAIR = 2 * HEAD_DIM
EPS = 1e-06
SCALE = HEAD_DIM ** (-0.5)
CHUNKS = 4
VMEM_BYTES = 56 * 1024 * 1024

bf16 = jnp.bfloat16
f32 = jnp.float32
MESH = pl.DeviceIdType.MESH


def chip_grid(count):
    for side in range(1, count + 1):
        if 2 * side**3 == count:
            return (2 * side, side, side)
    return (count, 1, 1)


def place(dims):
    me = lax.axis_index("dp")
    _, size_y, size_x = dims
    return me // (size_y * size_x), (me // size_x) % size_y, me % size_x


def rank(dims, z, y, x):
    return (z * dims[1] + y) * dims[2] + x


def greet(dims, s, z, y, x):
    barrier = pltpu.get_barrier_semaphore()
    count = 1
    pl.semaphore_signal(barrier, inc=1, device_id={"section": 1 - s}, device_id_type=MESH)
    for axis, (size, at) in enumerate(zip(dims, (z, y, x))):
        for d in range(1, size):
            there = [z, y, x]
            there[axis] = (at + d) % size
            pl.semaphore_signal(barrier, inc=1, device_id={"dp": rank(dims, *there)}, device_id_type=MESH)
            count += 1
    pl.semaphore_wait(barrier, count)


def row_chunks(rows):
    tiles = rows // 16
    parts = min(CHUNKS, tiles)
    cuts = [16 * (tiles * i // parts) for i in range(parts + 1)]
    return [(low, high - low) for low, high in zip(cuts, cuts[1:])]


def selector(tall, wide, offset):
    row = lax.broadcasted_iota(jnp.int32, (tall, wide), 0)
    col = lax.broadcasted_iota(jnp.int32, (tall, wide), 1)
    return jnp.where(col == row + offset, 1.0, 0.0).astype(f32)


def build_shard(dims, vec_ref, bias_ref, qkv_ref, wo_ref, up_ref, down_ref, shard):
    per, width = wo_ref.shape
    ff_per = down_ref.shape[0]
    me = lax.axis_index("dp")
    ups = up_ref.shape[1] // width
    pieces = [qkv_ref[:, i * width:(i + 1) * width] for i in range(3)] + [wo_ref[...]]
    pieces += [up_ref[:, i * width:(i + 1) * width] for i in range(ups)]
    for i in range(0, len(pieces), 2):
        both = jnp.concatenate([pieces[i].astype(f32), pieces[i + 1].astype(f32)], axis=0)
        shard[i * per:(i + 2) * per] = both.astype(bf16)
    top = len(pieces) * per
    shard[top:top + ff_per] = down_ref[...]
    shard[top + ff_per:] = build_tail(me, vec_ref[...], bias_ref[...], ups, width).astype(bf16)


def build_tail(me, vec, bias, ups, width):
    per, ff_per = vec.shape[1], bias.shape[1]
    put = jnp.dot(vec.astype(f32), selector(per, width, me * per), preferred_element_type=f32)
    line = jnp.dot(jnp.broadcast_to(bias.astype(f32), (8, ff_per)), selector(ff_per, width, (me * ff_per) % width),
                   preferred_element_type=f32)
    at = lax.broadcasted_iota(jnp.int32, (8, width), 0)
    return jnp.concatenate([put, jnp.where(at == (me * ff_per) // width, line, 0.0)], axis=0)


def gather_kernel(dims, fast, *refs):
    if fast:
        vec_ref, bias_ref, qkv_ref, wo_ref, up_ref, down_ref, img_ref, out_ref, img_out, shard_ref = refs[:10]
    else:
        shard_ref, img_ref, out_ref, img_out = refs[:4]
    own_sem, img_sems, send_sems, recv_sems, core_send, core_recv = refs[-6:]
    size_z, side, _ = dims
    s = lax.axis_index("section")
    z, y, x = place(dims)
    if fast:
        build_shard(dims, vec_ref, bias_ref, qkv_ref, wo_ref, up_ref, down_ref, shard_ref)
    rows = shard_ref.shape[0]
    greet(dims, s, z, y, x)
    waiting = []
    arriving = []
    counter = [0, 0]

    def remote(src, dst, there):
        slot = counter[0]
        counter[0] += 1
        copy = pltpu.make_async_remote_copy(
            src_ref=src, dst_ref=dst, send_sem=send_sems.at[slot], recv_sem=recv_sems.at[slot],
            device_id={"dp": rank(dims, *there)}, device_id_type=MESH,
        )
        copy.start()
        waiting.append(copy)
        return copy

    def to_core(*at):
        slot = counter[1]
        counter[1] += 1
        for section, do_start in ((s, True), (1 - s, False)):
            piece = out_ref.at[(section,) + at]
            copy = pltpu.make_async_remote_copy(
                src_ref=piece, dst_ref=piece, send_sem=core_send.at[slot], recv_sem=core_recv.at[slot],
                device_id={"section": 1 - s}, device_id_type=MESH,
            )
            if do_start:
                copy.start()
                waiting.append(copy)
            else:
                arriving.append(copy)

    image = pltpu.make_async_remote_copy(
        src_ref=img_ref.at[1 - s], dst_ref=img_out, send_sem=img_sems.at[0], recv_sem=img_sems.at[1],
        device_id={"section": 1 - s}, device_id_type=MESH,
    )
    every = slice(None)
    chunks = [pl.ds(low, size) for low, size in row_chunks(rows)]
    first = []
    for part in chunks:
        first.append([
            (remote(shard_ref.at[part], out_ref.at[s, z, y, x, part], ((z + d) % size_z, y, x)), (z - d + size_z) % size_z)
            for d in range(1, size_z)
        ])
    own = pltpu.make_async_copy(shard_ref, out_ref.at[s, z, y, x], own_sem)
    own.start()
    image.start()
    own.wait()
    to_core(z, y, x)

    second, third = {}, {}
    for t in range(len(chunks) + 2):
        if t < len(chunks):
            part = chunks[t]
            for copy, from_z in first[t]:
                copy.wait_recv()
                to_core(from_z, y, x, part)
            piece = out_ref.at[s, every, y, x, part]
            second[t] = []
            for d in range(1, side):
                if t % 2 == 0:
                    second[t].append((remote(piece, piece, (z, (y + d) % side, x)), (y - d + side) % side))
                else:
                    second[t].append((remote(piece, piece, (z, y, (x + d) % side)), (x - d + side) % side))
        c = t - 1
        if 0 <= c < len(chunks):
            part = chunks[c]
            for copy, at in second[c]:
                copy.wait_recv()
                if c % 2 == 0:
                    to_core(every, at, x, part)
                else:
                    to_core(every, y, at, part)
            third[c] = []
            for d in range(1, side):
                if c % 2 == 0:
                    piece = out_ref.at[s, every, every, x, part]
                    third[c].append((remote(piece, piece, (z, y, (x + d) % side)), (x - d + side) % side))
                else:
                    piece = out_ref.at[s, every, y, every, part]
                    third[c].append((remote(piece, piece, (z, (y + d) % side, x)), (y - d + side) % side))
        c = t - 2
        if 0 <= c < len(chunks):
            part = chunks[c]
            for copy, at in third[c]:
                copy.wait_recv()
                if c % 2 == 0:
                    to_core(every, every, at, part)
                else:
                    to_core(every, at, every, part)
    for copy in waiting:
        copy.wait_send()
    for copy in arriving:
        copy.wait_recv()
    image.wait()


def gather(dims, fast, sources, images, rows, width):
    size_z, side, _ = dims
    parts = len(row_chunks(rows))
    across = parts * ((size_z - 1) + 2 * (side - 1))
    any_spec = pl.BlockSpec(memory_space=pl.ANY)
    vmem = pl.BlockSpec(memory_space=pltpu.VMEM)
    sems = [
        pltpu.SemaphoreType.DMA,
        pltpu.SemaphoreType.DMA((2,)),
        pltpu.SemaphoreType.DMA((max(across, 1),)),
        pltpu.SemaphoreType.DMA((max(across, 1),)),
        pltpu.SemaphoreType.DMA((across + 1,)),
        pltpu.SemaphoreType.DMA((across + 1,)),
    ]
    return pl.pallas_call(
        functools.partial(gather_kernel, dims, fast),
        out_shape=(
            jax.ShapeDtypeStruct((2,) + dims + (rows, width), bf16),
            jax.ShapeDtypeStruct(images.shape[1:], bf16),
        ),
        in_specs=[vmem] * len(sources) + [any_spec] if fast else [any_spec] * 2,
        out_specs=(any_spec, any_spec),
        scratch_shapes=([pltpu.VMEM((rows, width), bf16)] if fast else []) + sems,
        compiler_params=pltpu.CompilerParams(collective_id=0, has_side_effects=True, vmem_limit_bytes=VMEM_BYTES),
        name="weight_gather",
    )(*sources, images)


def scatter_kernel(dims, part_ref, rows_ref, *refs):
    outs, rows_out = refs[:-14], refs[-14]
    (core_in, work, in_one, two, in_two, three, in_three, total_s,
     row_sems, send_sems, recv_sems, core_send, core_recv) = refs[-13:]
    size_z, side, _ = dims
    s = lax.axis_index("section")
    z, y, x = place(dims)
    rows = total_s.shape[0]
    every = slice(None)
    greet(dims, s, z, y, x)
    waiting = []
    counter = [0]

    def remote(src, dst, there):
        slot = counter[0]
        counter[0] += 1
        copy = pltpu.make_async_remote_copy(
            src_ref=src, dst_ref=dst, send_sem=send_sems.at[slot], recv_sem=recv_sems.at[slot],
            device_id={"dp": rank(dims, *there)}, device_id_type=MESH,
        )
        copy.start()
        waiting.append(copy)
        return copy

    chunks = [pl.ds(low, size) for low, size in row_chunks(rows)]
    cores = []
    for slot, part in enumerate(chunks):
        copy = pltpu.make_async_remote_copy(
            src_ref=part_ref.at[1 - s, :, :, :, part], dst_ref=core_in.at[:, :, :, part],
            send_sem=core_send.at[slot], recv_sem=core_recv.at[slot],
            device_id={"section": 1 - s}, device_id_type=MESH,
        )
        copy.start()
        cores.append(copy)
    row_copy = pltpu.make_async_remote_copy(
        src_ref=rows_ref.at[s], dst_ref=rows_out, send_sem=row_sems.at[0], recv_sem=row_sems.at[1],
        device_id={"section": 1 - s}, device_id_type=MESH,
    )
    row_copy.start()

    def step_core(c):
        part = chunks[c]
        cores[c].wait_recv()

        @pl.loop(0, size_z * side * side)
        def _(i):
            u, v, w = i // (side * side), (i // side) % side, i % side
            work[u, v, w, part] = (part_ref[s, u, v, w, part].astype(f32) + core_in[u, v, w, part].astype(f32)).astype(bf16)

        sent = []
        for d in range(1, side):
            if c % 2 == 0:
                at = (x + d) % side
                sent.append(remote(work.at[:, :, at, part], in_one.at[d - 1, :, :, part], (z, y, at)))
            else:
                at = (y + d) % side
                sent.append(remote(work.at[:, at, :, part], in_one.at[d - 1, :, :, part], (z, at, x)))
        return sent

    def step_one(c, sent):
        part = chunks[c]
        for copy in sent:
            copy.wait_recv()

        @pl.loop(0, size_z * side)
        def _(i):
            u, v = i // side, i % side
            at = (u, v, x) if c % 2 == 0 else (u, y, v)
            total = work[at + (part,)].astype(f32)
            for d in range(1, side):
                total = total + in_one[d - 1, u, v, part].astype(f32)
            two[v, u, part] = total.astype(bf16)

        sent = []
        for d in range(1, side):
            at = ((y if c % 2 == 0 else x) + d) % side
            there = (z, at, x) if c % 2 == 0 else (z, y, at)
            sent.append(remote(two.at[at, :, part], in_two.at[d - 1, :, part], there))
        return sent

    def step_two(c, sent):
        part = chunks[c]
        for copy in sent:
            copy.wait_recv()

        @pl.loop(0, size_z)
        def _(u):
            total = two[y if c % 2 == 0 else x, u, part].astype(f32)
            for d in range(1, side):
                total = total + in_two[d - 1, u, part].astype(f32)
            three[u, part] = total.astype(bf16)

        return [
            remote(three.at[(z + d) % size_z, part], in_three.at[d - 1, part], ((z + d) % size_z, y, x))
            for d in range(1, size_z)
        ]

    def step_three(c, sent):
        part = chunks[c]
        for copy in sent:
            copy.wait_recv()
        total = three[z, part].astype(f32)
        for d in range(1, size_z):
            total = total + in_three[d - 1, part].astype(f32)
        total_s[part] = total

    one, again, last = {}, {}, {}
    for t in range(len(chunks) + 3):
        if t < len(chunks):
            one[t] = step_core(t)
        if 0 <= t - 1 < len(chunks):
            again[t - 1] = step_one(t - 1, one[t - 1])
        if 0 <= t - 2 < len(chunks):
            last[t - 2] = step_two(t - 2, again[t - 2])
        if 0 <= t - 3 < len(chunks):
            step_three(t - 3, last[t - 3])
    if len(outs) == 1:
        outs[0][...] = total_s[...]
    else:
        qkv_out, wo_out, up_out, down_out, tail_out = outs
        per, width = wo_out.shape
        spots = [(qkv_out, i) for i in range(3)] + [(wo_out, 0)] + [(up_out, i) for i in range(up_out.shape[1] // width)]
        for i, (ref, j) in enumerate(spots):
            ref[:, j * width:(j + 1) * width] = total_s[i * per:(i + 1) * per]
        top = len(spots) * per
        down_out[...] = total_s[top:top + down_out.shape[0]]
        tail_out[...] = total_s[top + down_out.shape[0]:]
    for copy in waiting + cores:
        copy.wait_send()
    row_copy.wait()


def scatter(dims, partials, rows_pair, out_shapes):
    rows, width = partials.shape[-2:]
    size_z, side, _ = dims
    parts = len(row_chunks(rows))
    across = max(parts * ((size_z - 1) + 2 * (side - 1)), 1)
    more = max(side - 1, 1)
    vmem = pl.BlockSpec(memory_space=pltpu.VMEM)
    any_spec = pl.BlockSpec(memory_space=pl.ANY)
    return pl.pallas_call(
        functools.partial(scatter_kernel, dims),
        out_shape=tuple(jax.ShapeDtypeStruct(shape, f32) for shape in out_shapes)
        + (jax.ShapeDtypeStruct(rows_pair.shape[1:], bf16),),
        in_specs=[vmem, any_spec],
        out_specs=(vmem,) * len(out_shapes) + (any_spec,),
        scratch_shapes=[
            pltpu.VMEM(dims + (rows, width), bf16),
            pltpu.VMEM(dims + (rows, width), bf16),
            pltpu.VMEM((more, size_z, side, rows, width), bf16),
            pltpu.VMEM((side, size_z, rows, width), bf16),
            pltpu.VMEM((more, size_z, rows, width), bf16),
            pltpu.VMEM((size_z, rows, width), bf16),
            pltpu.VMEM((max(size_z - 1, 1), rows, width), bf16),
            pltpu.VMEM((rows, width), f32),
            pltpu.SemaphoreType.DMA((2,)),
            pltpu.SemaphoreType.DMA((across,)),
            pltpu.SemaphoreType.DMA((across,)),
            pltpu.SemaphoreType.DMA((parts,)),
            pltpu.SemaphoreType.DMA((parts,)),
        ],
        compiler_params=pltpu.CompilerParams(collective_id=1, has_side_effects=True, vmem_limit_bytes=VMEM_BYTES),
        name="grad_scatter",
    )(partials, rows_pair)


def mm(left, right):
    return jnp.dot(left, right, preferred_element_type=f32)


def mm_t(left, right):
    return lax.dot_general(left, right, (((1,), (1,)), ((), ())), preferred_element_type=f32)


def t_mm(left, right):
    return lax.dot_general(left, right, (((0,), (0,)), ((), ())), preferred_element_type=f32)


def norm_parts(values):
    average = jnp.mean(values, axis=-1, keepdims=True)
    centered = values - average
    inverse = lax.rsqrt(jnp.mean(centered * centered, axis=-1, keepdims=True) + EPS)
    return centered * inverse, inverse


def norm_back(unit, inverse, gain, grad):
    scaled = grad * (1.0 + gain)
    mean_one = jnp.mean(scaled, axis=-1, keepdims=True)
    mean_two = jnp.mean(scaled * unit, axis=-1, keepdims=True)
    return (
        inverse * (scaled - mean_one - unit * mean_two),
        jnp.sum(grad * unit, axis=0, keepdims=True),
        jnp.sum(grad, axis=0, keepdims=True),
    )


def layers_kernel(seq, per, ff_per, rows_ref, cot_ref, *refs):
    fast = per is not None
    if fast:
        blocks_ref, out_ref, parts_ref, w_s, tail_s, f_s = refs[:6]
    else:
        w_s, down_all, tail_s, out_ref, gw_ref, gdown_ref, gtail_ref = refs[:7]
    h_s, a_s, q_s, o_s, z_s, n_s, g_s, slope_s, pf_s, dn_s, dy_s, dqkv_s, gt_s = refs[-13:]
    rows, width = cot_ref.shape
    ff = g_s.shape[-1]
    kinds = w_s.shape[1]
    down_at = kinds * per if fast else 0

    def down_part(e, c):
        if fast:
            group = width // ff_per
            return blocks_ref[e, c * group:(c + 1) * group, down_at:down_at + ff_per].reshape(width, width)
        return down_all[e, c * width:(c + 1) * width]

    def keep_grad(e, kind, value):
        if fast:
            f_s[kind] = value
        else:
            gw_ref[e, kind] = value.astype(bf16)

    def keep_down(e, c, value):
        if fast:
            group = width // ff_per
            for i in range(group):
                parts_ref[e, c * group + i, down_at:down_at + ff_per] = value[i * ff_per:(i + 1) * ff_per].astype(bf16)
        else:
            gdown_ref[e, c * width:(c + 1) * width] = value.astype(bf16)

    if fast:
        count = blocks_ref.shape[1]
        for e in range(2):
            tail_s[e] = jnp.zeros(tail_s.shape[1:], f32)

            @pl.loop(0, count // 2)
            def _(m, e=e):
                left = blocks_ref[e, 2 * m, 0:down_at].astype(f32)
                right = blocks_ref[e, 2 * m + 1, 0:down_at].astype(f32)
                at = pl.ds(pl.multiple_of(2 * per * m, 2 * per), 2 * per)
                for kind in range(kinds):
                    piece = slice(kind * per, (kind + 1) * per)
                    w_s[e, kind, at] = jnp.concatenate([left[piece], right[piece]], axis=0).astype(bf16)
                tail_s[e] += (
                    blocks_ref[e, 2 * m, down_at + ff_per:].astype(f32)
                    + blocks_ref[e, 2 * m + 1, down_at + ff_per:].astype(f32)
                )
    pairs = width // PAIR
    lane = lax.broadcasted_iota(jnp.int32, (rows, PAIR), 1)
    low_half = lane < HEAD_DIM
    key_ok = lax.broadcasted_iota(jnp.int32, (rows, rows), 1) < seq
    zero = jnp.zeros((rows, PAIR), bf16)

    def halves(values):
        return jnp.where(low_half, values, zero), jnp.where(low_half, zero, values)

    h_s[0] = rows_ref[...].astype(f32)

    @pl.loop(0, 2)
    def _(e):
        vec = tail_s[e, 0:8]
        bias = tail_s[e, 8:16]
        h = h_s[e]
        unit, _ = norm_parts(h)
        a = (unit * (1.0 + vec[0:1]) + vec[1:2]).astype(bf16)
        a_s[e] = a
        for third in range(3):
            cols = slice(third * width, (third + 1) * width)
            part = mm(a, w_s[e, third])
            if third != 1:
                part = part + vec[2 + third // 2:3 + third // 2]
            q_s[e, :, cols] = part.astype(bf16)
        for j in range(pairs):
            q = q_s[e, :, j * PAIR:(j + 1) * PAIR]
            k = q_s[e, :, width + j * PAIR:width + (j + 1) * PAIR]
            v = q_s[e, :, 2 * width + j * PAIR:2 * width + (j + 1) * PAIR]
            outs = []
            for i, q_half in enumerate(halves(q)):
                scores = jnp.where(key_ok, mm_t(q_half, k) * SCALE, -1e30)
                shifted = jnp.exp(scores - jnp.max(scores, axis=-1, keepdims=True))
                pf = shifted / jnp.sum(shifted, axis=-1, keepdims=True)
                pf_s[e, 2 * j + i] = pf
                outs.append(mm(pf.astype(bf16), v))
            o_s[e, :, j * PAIR:(j + 1) * PAIR] = jnp.where(low_half, outs[0], outs[1]).astype(bf16)
        z = h + mm(o_s[e], w_s[e, 3]) + vec[4:5]
        z_s[e] = z
        unit, _ = norm_parts(z)
        n = (unit * (1.0 + vec[5:6]) + vec[6:7]).astype(bf16)
        n_s[e] = n
        for c in range(ff // width):
            cols = slice(c * width, (c + 1) * width)
            u = mm(n, w_s[e, 4 + c]) + bias[c:c + 1]
            phi = 0.5 + 0.5 * lax.erf(u * (0.5 ** 0.5))
            g_s[e, :, cols] = (u * phi).astype(bf16)
            slope_s[e, :, cols] = phi + u * (jnp.exp(-0.5 * u * u) * 0.3989422804014327)
        total = z + vec[7:8]
        for c in range(ff // width):
            total = total + mm(g_s[e, :, c * width:(c + 1) * width], down_part(e, c))
        result = total.astype(bf16)
        out_ref[0] = result
        h_s[1] = jnp.where(e == 0, result.astype(f32), h_s[1])

    dy_s[...] = cot_ref[...].astype(f32)

    @pl.loop(0, 2)
    def _(step):
        e = 1 - step
        vec = tail_s[e, 0:8]
        dy = dy_s[...]
        dm = dy.astype(bf16)
        g7 = jnp.sum(dm.astype(f32), axis=0, keepdims=True)
        n = n_s[e]
        for c in range(ff // width):
            cols = slice(c * width, (c + 1) * width)
            keep_down(e, c, t_mm(g_s[e, :, cols], dm))
            du = (mm_t(dm, down_part(e, c)) * slope_s[e, :, cols]).astype(bf16)
            gt_s[8 + c:9 + c] = jnp.sum(du.astype(f32), axis=0, keepdims=True)
            keep_grad(e, 4 + c, t_mm(n, du))
            back = mm_t(du, w_s[e, 4 + c])
            if c == 0:
                dn_s[...] = back
            else:
                dn_s[...] += back
        unit, inverse = norm_parts(z_s[e])
        dz, g5, g6 = norm_back(unit, inverse, vec[5:6], dn_s[...])
        dz = dz + dy
        dr = dz.astype(bf16)
        g4 = jnp.sum(dr.astype(f32), axis=0, keepdims=True)
        keep_grad(e, 3, t_mm(o_s[e], dr))
        do_all = mm_t(dr, w_s[e, 3]).astype(bf16)
        for j in range(pairs):
            q = q_s[e, :, j * PAIR:(j + 1) * PAIR]
            k = q_s[e, :, width + j * PAIR:width + (j + 1) * PAIR]
            v = q_s[e, :, 2 * width + j * PAIR:2 * width + (j + 1) * PAIR]
            do = do_all[:, j * PAIR:(j + 1) * PAIR]
            dq, dk, dv = [], [], []
            for i, do_half in enumerate(halves(do)):
                pf = pf_s[e, 2 * j + i]
                dp = mm_t(do_half, v)
                ds = (pf * (dp - jnp.sum(pf * dp, axis=-1, keepdims=True))).astype(bf16)
                dv.append(t_mm(pf.astype(bf16), do))
                dq.append(mm(ds, k))
                dk.append(t_mm(ds, q))
            dqkv_s[:, j * PAIR:(j + 1) * PAIR] = (jnp.where(low_half, dq[0], dq[1]) * SCALE).astype(bf16)
            dqkv_s[:, width + j * PAIR:width + (j + 1) * PAIR] = (jnp.where(low_half, dk[0], dk[1]) * SCALE).astype(bf16)
            dqkv_s[:, 2 * width + j * PAIR:2 * width + (j + 1) * PAIR] = jnp.where(low_half, dv[0], dv[1]).astype(bf16)
        a = a_s[e]
        sums = []
        for third in range(3):
            cols = slice(third * width, (third + 1) * width)
            dpart = dqkv_s[:, cols]
            sums.append(jnp.sum(dpart.astype(f32), axis=0, keepdims=True))
            keep_grad(e, third, t_mm(a, dpart))
            back = mm_t(dpart, w_s[e, third])
            if third == 0:
                dn_s[...] = back
            else:
                dn_s[...] += back
        unit, inverse = norm_parts(h_s[e])
        dh, g0, g1 = norm_back(unit, inverse, vec[0:1], dn_s[...])
        low = (dz + dh).astype(bf16)
        out_ref[1] = low
        dy_s[...] = low.astype(f32)
        for row, value in enumerate((g0, g1, sums[0], sums[2], g4, g5, g6, g7)):
            gt_s[row:row + 1] = value
        if not fast:
            gtail_ref[e] = gt_s[...]
        else:
            @pl.loop(0, parts_ref.shape[1])
            def _(k):
                at = pl.ds(pl.multiple_of(per * k, per), per)
                for kind in range(0, kinds, 2):
                    both = jnp.concatenate([f_s[kind, at], f_s[kind + 1, at]], axis=0)
                    parts_ref[e, k, kind * per:(kind + 2) * per] = both.astype(bf16)
                parts_ref[e, k, down_at + ff_per:] = gt_s[...].astype(bf16)


def run_layers(seq, per, ff_per, rows, cot, weights, kinds, ff):
    t, width = rows.shape
    fast = per is not None
    vmem = pl.BlockSpec(memory_space=pltpu.VMEM)
    shape = jax.ShapeDtypeStruct
    outs = [shape((2, t, width), bf16)]
    outs += [shape(item.shape, bf16) for item in weights[:2]]
    if not fast:
        outs.append(shape(weights[2].shape, f32))
    extra = [
        pltpu.VMEM((2, kinds, width, width), bf16),
        pltpu.VMEM((2, 16, width), f32),
        pltpu.VMEM((kinds, width, width), f32),
    ]
    return pl.pallas_call(
        functools.partial(layers_kernel, seq, per, ff_per),
        out_shape=tuple(outs),
        in_specs=[vmem] * (2 + len(weights)),
        out_specs=(vmem,) * len(outs),
        scratch_shapes=(extra if fast else []) + [
            pltpu.VMEM((2, t, width), f32),
            pltpu.VMEM((2, t, width), bf16),
            pltpu.VMEM((2, t, 3 * width), bf16),
            pltpu.VMEM((2, t, width), bf16),
            pltpu.VMEM((2, t, width), f32),
            pltpu.VMEM((2, t, width), bf16),
            pltpu.VMEM((2, t, ff), bf16),
            pltpu.VMEM((2, t, ff), f32),
            pltpu.VMEM((2, HEADS, t, t), f32),
            pltpu.VMEM((t, width), f32),
            pltpu.VMEM((t, width), f32),
            pltpu.VMEM((t, 3 * width), bf16),
            pltpu.VMEM((16, width), f32),
        ],
        compiler_params=pltpu.CompilerParams(vmem_limit_bytes=VMEM_BYTES),
        name="two_layers",
    )(rows, cot, *weights)


def pack(count, pieces, down, tail):
    lead, kinds, width = pieces.shape[:-3], pieces.shape[-3], pieces.shape[-1]
    pieces = jnp.moveaxis(pieces.reshape(lead + (kinds, count, -1, width)), -4, -3)
    down = down.reshape(lead + (count, -1, width))
    tail = tail if tail.ndim == down.ndim else jnp.broadcast_to(tail[..., None, :, :], down.shape[:-2] + tail.shape[-2:])
    blocks = jnp.concatenate([pieces.reshape(lead + (count, -1, width)), down, tail.astype(bf16)], axis=-2)
    return jnp.pad(blocks, [(0, 0)] * (blocks.ndim - 2) + [(0, -blocks.shape[-2] % 16), (0, 0)])


def unpack(blocks, kinds, per, ff_per):
    lead, (count, _, width) = blocks.shape[:-3], blocks.shape[-3:]
    top = kinds * per
    pieces = blocks[..., :top, :].reshape(lead + (count, kinds, per, width))
    pieces = jnp.moveaxis(pieces, -3, -4).reshape(lead + (kinds, count * per, width))
    down = blocks[..., top:top + ff_per, :].reshape(lead + (count * ff_per, width))
    return pieces, down, blocks[..., top + ff_per:top + ff_per + 16, :]


def shards(dims, ends_in, vectors, up_bias, w_qkv, w_out, w_up, w_down):
    section_id = lax.axis_index("section")
    me = lax.axis_index("dp")
    is_first = section_id == 0
    local = ends_in[0]
    _, seq, width = local.shape
    count = dims[0] * dims[1] * dims[2]
    vec_rows, per = vectors.shape[1:]
    ff_per = up_bias.shape[1]
    ff = ff_per * count
    ups = ff // width
    kinds = 4 + ups
    fast = per % 8 == 0 and ff_per % 16 == 0 and width % ff_per == 0 and kinds % 2 == 0 and count % 2 == 0
    used = kinds * per + ff_per + 16
    rows = -(-used // 16) * 16
    t = -(-seq // 16) * 16
    padded = jnp.pad(local, ((0, 0), (0, t - seq), (0, 0)))

    def columns(matrix):
        return jnp.moveaxis(matrix.reshape(matrix.shape[0], -1, width), 1, 0)

    if fast:
        sources = (vectors[0], up_bias, w_qkv[0], w_out[0], w_up[0], w_down[0])
    else:
        tail = build_tail(me, vectors[0], up_bias, ups, width)
        pieces = jnp.concatenate([columns(w_qkv[0]), w_out[0][None], columns(w_up[0])])
        sources = (pack(1, pieces, w_down[0], tail)[0],)
    blocks, other = gather(dims, fast, sources, padded, rows, width)
    blocks = blocks.reshape(2, count, rows, width)
    own = lax.dynamic_index_in_dim(padded, section_id, 0, keepdims=False)
    x_rows = jnp.where(is_first, own, other)
    cot = jnp.where(is_first, other, own)
    if fast:
        pair, partials = run_layers(seq, per, ff_per, x_rows, cot, (blocks,), kinds, ff)
    else:
        pieces, down, tails = unpack(blocks, kinds, per, ff_per)
        tail = jnp.sum(tails.astype(f32), axis=1)
        pair, gpieces, gdown, gtail = run_layers(seq, None, None, x_rows, cot, (pieces, down, tail), kinds, ff)
        partials = pack(count, gpieces, gdown, gtail)
    partials = partials.reshape((2,) + dims + (rows, width))
    if fast:
        shapes = ((per, 3 * width), (per, width), (per, ff), (ff_per, width), (16, width))
        fqkv, fwo, fup, fdown, ftail, got = scatter(dims, partials, pair, shapes)
    else:
        total, got = scatter(dims, partials, pair, ((rows, width),))
        pieces, fdown, ftail = unpack(total[None], kinds, per, ff_per)
        ftail = ftail[0]
        fqkv = jnp.moveaxis(pieces[:3], 0, 1).reshape(per, 3 * width)
        fwo = pieces[3]
        fup = jnp.moveaxis(pieces[4:], 0, 1).reshape(per, ff)
    fvec = lax.dynamic_slice_in_dim(ftail[:vec_rows], me * per, per, 1)
    fbias = lax.dynamic_slice_in_dim(ftail[8:8 + ups].reshape(-1), me * ff_per, ff_per, 0)
    ends = jnp.stack([jnp.where(is_first, pair[1], got), jnp.where(is_first, got, pair[0])])[None, :, :seq]
    return ends, fvec[None], fbias[None], fqkv[None], fwo[None], fup[None], fdown[None]


def solution(mesh):
    dims = chip_grid(mesh.shape["dp"])
    specs = (
        P("section", "dp", None, None),
        P("section", None, "dp"),
        P("section", "dp"),
        P("section", "dp", None),
        P("section", "dp", None),
        P("section", "dp", None),
        P("section", "dp", None),
    )
    return jax.shard_map(
        functools.partial(shards, dims), mesh=mesh, in_specs=specs, out_specs=specs, check_vma=False
    )
```

time: 206 us -> 154 us (0.75)
  local copies, waits for them, and re-layouts: 49 us -> 11.5 us
  Pallas kernels: 149 us -> 137 us
    reshape x12 -> x1, local copies, waits for them, and re-layouts: 14.9 us -> 0.01 us  [shards(): ftail[8:8 + ups].reshape(-1)]
    pallas_call x3, Pallas kernels: 149 us -> 137 us  [the longest x1 58.3 us: scatter(): pl.pallas_call(functools.partial(scatter_kernel, dims), out_shape=tuple((...]
    slice x9 -> x2, local copies, waits for them, and re-layouts: 13.6 us -> 1.42 us  [the longest x1 0.71 us: shards(): fvec = lax.dynamic_slice_in_dim(ftail[:vec_rows], me * per, per, 1)]
    another operation x6 -> x0, local copies, waits for them, and re-layouts: 4.54 us -> none  [the longest x2 1.72 us: split_cols(): matrix.reshape(lead + (count, per, across, width))]
    unnamed x27 -> x8, local copies, waits for them, and re-layouts: 11.6 us -> 8.05 us
where the time goes in v2:
time: 154 us; the launch traced here: 152 us
  Pallas kernels  137 us (89%)
  local copies, waits for them, and re-layouts  11.5 us (7%)
  other arithmetic  2.67 us (2%)
    pallas_call x1, Pallas kernels, scatter(): pl.pallas_call(functools.partial(scatter_kernel, dims), out_shape=tuple((...  58.3 us
    pallas_call x1, Pallas kernels, gather(): pl.pallas_call(functools.partial(gather_kernel, dims, fast), out_shape=(j...  53.4 us
    pallas_call x1, Pallas kernels, run_layers(): pl.pallas_call(functools.partial(layers_kernel, seq, per, ff_per), out_sh...  25.3 us
    unnamed x8, local copies, waits for them, and re-layouts  8.05 us

profile of v2, /device:TPU:0, one launch (start us, length us, event | category | flops | bytes accessed | tf_op | source)
XLA Modules:
  0.0 151.9 jit_solution(10008217240793006167)
XLA Ops:
  0.6 1.0 copy.17
  1.6 0.7 pad.4.refs_6_
  2.4 53.4 %weight_gather.1 = (bf16[2,4,2,2,304,384]{5,4,3,2,1,0:T(8,128)(2,1)}, bf16[208,384]{1,0:T(8,128)(2,1)}) custom-call(bf16[8,24]{1,0:T(8,128)(2,1)} %bitcast.47, bf16[1,96]{1,0:T(2,128)(2,1)} %refs_1_.1, bf16[24,1152]{1,0:T(8,128)(2,1)} %bitcast.44, bf16[24,384]{1,0:T(8,128)(2,1)} %bitcast.46, bf16[24,1536]{1,0:T(8,128)(2,1)} %bitcast.42, ...), custom_call_target="tpu_custom_call" | custom-call | tf_op jit(solution)/shard_map/weight_gather/pallas_call | solution.py:212
  55.8 1.7 %bitcast_select_fusion.2 = (bf16[208,384]{1,0:T(8,128)(2,1)}, bf16[208,384]{1,0:T(8,128)(2,1)}) fusion(bf16[208,384]{1,0:T(8,128)(2,1)} %get-tuple-element.17, pred[]{:T(512)S(6)} %eq.3, s32[]{:T(128)S(6)} %select_n.31, bf16[2,197,384]{2,1,0:T(8,128)(2,1)S(1)} %bitcast.38), kind=kLoop, calls=%fused_computation.7 | loop fusion | flops 159744 | bytes 781829 | tf_op jit(solution)/shard_map/jit(_where)/select_n | solution.py:689
  57.5 25.3 %two_layers.1 = (bf16[2,208,384]{2,1,0:T(8,128)(2,1)}, bf16[2,16,304,384]{3,2,1,0:T(8,128)(2,1)}) custom-call(bf16[208,384]{1,0:T(8,128)(2,1)} %get-tuple-element.37.rows_ref, bf16[208,384]{1,0:T(8,128)(2,1)} %get-tuple-element.36.cot_ref, bf16[2,16,304,384]{3,2,1,0:T(8,128)(2,1)} %bitcast.35), custom_call_target="tpu_custom_call" | custom-call | tf_op jit(solution)/shard_map/two_layers/pallas_call | solution.py:615
  82.8 0.0 copy-start
  82.8 58.3 %grad_scatter.1 = (f32[24,1152]{1,0:T(8,128)}, f32[24,384]{1,0:T(8,128)}, f32[24,1536]{1,0:T(8,128)}, f32[96,384]{1,0:T(8,128)}, f32[16,384]{1,0:T(8,128)}, /*index=5*/bf16[208,384]{1,0:T(8,128)(2,1)}) custom-call(bf16[2,4,2,2,304,384]{5,4,3,2,1,0:T(8,128)(2,1)} %bitcast.36, bf16[2,208,384]{2,1,0:T(8,128)(2,1)} %get-tuple-element.19.rows_ref), custom_call_target="tpu_custom_call" | custom-call | tf_op jit(solution)/shard_map/grad_scatter/pallas_call | solution.py:366
  141.1 0.0 copy-done
  141.1 1.0 fusion.2
  142.1 1.0 copy.15
  143.1 0.7 slice.18
  143.8 0.7 dynamic-slice_bitcast_fusion
  144.5 0.7 slice.19
  145.2 0.6 dynamic-slice_bitcast_fusion.1
  145.8 1.5 %copy.22 = f32[1,24,1152]{2,1,0:T(8,128)} copy(f32[1,24,1152]{2,1,0:T(8,128)} %bitcast.41) | data formatting | bytes 221184
  147.3 1.4 copy.23
  148.7 1.6 %copy.24 = f32[1,24,1536]{2,1,0:T(8,128)} copy(f32[1,24,1536]{2,1,0:T(8,128)} %bitcast.40) | data formatting | bytes 294912
  150.3 1.6 %copy.25 = f32[1,96,384]{2,1,0:T(8,128)} copy(f32[1,96,384]{2,1,0:T(8,128)} %bitcast.39) | data formatting | bytes 294912
  (2 shorter events, 0.0 us)
Async XLA Ops:
  82.8 58.3 %copy-start = (bf16[2,208,384]{2,1,0:T(8,128)(2,1)S(1)}, bf16[2,208,384]{2,1,0:T(8,128)(2,1)}, u32[]{:S(2)}) copy-start(bf16[2,208,384]{2,1,0:T(8,128)(2,1)} %get-tuple-element.19.rows_ref) | copy-start | bytes 958468

commit v3 on v2

--- a/solution.py
+++ b/solution.py
@@ -12,7 +12,9 @@
 PAIR = 2 * HEAD_DIM
 EPS = 1e-06
 SCALE = HEAD_DIM ** (-0.5)
-CHUNKS = 4
+GATHER_WEIGHTS = (1, 1)
+GATHER_DEPTH = 2
+SCATTER_WEIGHTS = (1, 1)
 VMEM_BYTES = 56 * 1024 * 1024
 
 bf16 = jnp.bfloat16
@@ -50,11 +52,20 @@
     pl.semaphore_wait(barrier, count)
 
 
-def row_chunks(rows):
-    tiles = rows // 16
-    parts = min(CHUNKS, tiles)
-    cuts = [16 * (tiles * i // parts) for i in range(parts + 1)]
-    return [(low, high - low) for low, high in zip(cuts, cuts[1:])]
+def row_groups(rows, weights):
+    tiles, total = rows // 16, sum(weights)
+    cuts = [tiles * sum(weights[:i]) // total for i in range(len(weights) + 1)]
+    groups = []
+    for low, high in zip(cuts, cuts[1:]):
+        middle = (low + high + len(groups) % 2) // 2
+        group = [(kind, pl.ds(16 * f, 16 * (l - f))) for kind, f, l in ((0, low, middle), (1, middle, high)) if l > f]
+        if group:
+            groups.append(group)
+    return groups
+
+
+def part_count(groups):
+    return sum(len(group) for group in groups)
 
 
 def selector(tall, wide, offset):
@@ -135,59 +146,56 @@
         device_id={"section": 1 - s}, device_id_type=MESH,
     )
     every = slice(None)
-    chunks = [pl.ds(low, size) for low, size in row_chunks(rows)]
-    first = []
-    for part in chunks:
-        first.append([
-            (remote(shard_ref.at[part], out_ref.at[s, z, y, x, part], ((z + d) % size_z, y, x)), (z - d + size_z) % size_z)
-            for d in range(1, size_z)
-        ])
+    groups = row_groups(rows, GATHER_WEIGHTS)
+
+    def send_z(group):
+        return [
+            (kind, part, (z - d + size_z) % size_z,
+             remote(shard_ref.at[part], out_ref.at[s, z, y, x, part], ((z + d) % size_z, y, x)))
+            for kind, part in group for d in range(1, size_z)
+        ]
+
+    first, second, third = {}, {}, {}
+    for c in range(min(GATHER_DEPTH, len(groups))):
+        first[c] = send_z(groups[c])
     own = pltpu.make_async_copy(shard_ref, out_ref.at[s, z, y, x], own_sem)
     own.start()
     image.start()
     own.wait()
     to_core(z, y, x)
-
-    second, third = {}, {}
-    for t in range(len(chunks) + 2):
-        if t < len(chunks):
-            part = chunks[t]
-            for copy, from_z in first[t]:
+    for t in range(len(groups) + 2):
+        if t < len(groups):
+            for kind, part, at, copy in first[t]:
                 copy.wait_recv()
-                to_core(from_z, y, x, part)
-            piece = out_ref.at[s, every, y, x, part]
+            if t + GATHER_DEPTH < len(groups):
+                first[t + GATHER_DEPTH] = send_z(groups[t + GATHER_DEPTH])
             second[t] = []
-            for d in range(1, side):
-                if t % 2 == 0:
-                    second[t].append((remote(piece, piece, (z, (y + d) % side, x)), (y - d + side) % side))
-                else:
-                    second[t].append((remote(piece, piece, (z, y, (x + d) % side)), (x - d + side) % side))
+            for kind, part in groups[t]:
+                piece = out_ref.at[s, every, y, x, part]
+                for d in range(1, side):
+                    there = (z, (y + d) % side, x) if kind == 0 else (z, y, (x + d) % side)
+                    at = ((y if kind == 0 else x) - d + side) % side
+                    second[t].append((kind, part, at, remote(piece, piece, there)))
+            for kind, part, at, copy in first[t]:
+                to_core(at, y, x, part)
         c = t - 1
-        if 0 <= c < len(chunks):
-            part = chunks[c]
-            for copy, at in second[c]:
+        if 0 <= c < len(groups):
+            for kind, part, at, copy in second[c]:
                 copy.wait_recv()
-                if c % 2 == 0:
-                    to_core(every, at, x, part)
-                else:
-                    to_core(every, y, at, part)
             third[c] = []
-            for d in range(1, side):
-                if c % 2 == 0:
-                    piece = out_ref.at[s, every, every, x, part]
-                    third[c].append((remote(piece, piece, (z, y, (x + d) % side)), (x - d + side) % side))
-                else:
-                    piece = out_ref.at[s, every, y, every, part]
-                    third[c].append((remote(piece, piece, (z, (y + d) % side, x)), (y - d + side) % side))
+            for kind, part in groups[c]:
+                piece = out_ref.at[s, every, every, x, part] if kind == 0 else out_ref.at[s, every, y, every, part]
+                for d in range(1, side):
+                    there = (z, y, (x + d) % side) if kind == 0 else (z, (y + d) % side, x)
+                    at = ((x if kind == 0 else y) - d + side) % side
+                    third[c].append((kind, part, at, remote(piece, piece, there)))
+            for kind, part, at, copy in second[c]:
+                to_core(*((every, at, x, part) if kind == 0 else (every, y, at, part)))
         c = t - 2
-        if 0 <= c < len(chunks):
-            part = chunks[c]
-            for copy, at in third[c]:
+        if 0 <= c < len(groups):
+            for kind, part, at, copy in third[c]:
                 copy.wait_recv()
-                if c % 2 == 0:
-                    to_core(every, every, at, part)
-                else:
-                    to_core(every, at, every, part)
+                to_core(*((every, every, at, part) if kind == 0 else (every, at, every, part)))
     for copy in waiting:
         copy.wait_send()
     for copy in arriving:
@@ -197,7 +205,7 @@
 
 def gather(dims, fast, sources, images, rows, width):
     size_z, side, _ = dims
-    parts = len(row_chunks(rows))
+    parts = part_count(row_groups(rows, GATHER_WEIGHTS))
     across = parts * ((size_z - 1) + 2 * (side - 1))
     any_spec = pl.BlockSpec(memory_space=pl.ANY)
     vmem = pl.BlockSpec(memory_space=pltpu.VMEM)
@@ -247,98 +255,105 @@
         waiting.append(copy)
         return copy
 
-    chunks = [pl.ds(low, size) for low, size in row_chunks(rows)]
+    groups = row_groups(rows, SCATTER_WEIGHTS)
     cores = []
-    for slot, part in enumerate(chunks):
-        copy = pltpu.make_async_remote_copy(
-            src_ref=part_ref.at[1 - s, :, :, :, part], dst_ref=core_in.at[:, :, :, part],
-            send_sem=core_send.at[slot], recv_sem=core_recv.at[slot],
-            device_id={"section": 1 - s}, device_id_type=MESH,
-        )
-        copy.start()
-        cores.append(copy)
+    for group in groups:
+        for kind, part in group:
+            slot = len(cores)
+            copy = pltpu.make_async_remote_copy(
+                src_ref=part_ref.at[1 - s, :, :, :, part], dst_ref=core_in.at[:, :, :, part],
+                send_sem=core_send.at[slot], recv_sem=core_recv.at[slot],
+                device_id={"section": 1 - s}, device_id_type=MESH,
+            )
+            copy.start()
+            cores.append(copy)
     row_copy = pltpu.make_async_remote_copy(
         src_ref=rows_ref.at[s], dst_ref=rows_out, send_sem=row_sems.at[0], recv_sem=row_sems.at[1],
         device_id={"section": 1 - s}, device_id_type=MESH,
     )
     row_copy.start()
-
-    def step_core(c):
-        part = chunks[c]
-        cores[c].wait_recv()
-
-        @pl.loop(0, size_z * side * side)
-        def _(i):
-            u, v, w = i // (side * side), (i // side) % side, i % side
-            work[u, v, w, part] = (part_ref[s, u, v, w, part].astype(f32) + core_in[u, v, w, part].astype(f32)).astype(bf16)
-
+    core_at = [0]
+
+    def step_core(group):
+        for kind, part in group:
+            cores[core_at[0]].wait_recv()
+            core_at[0] += 1
+
+            @pl.loop(0, size_z * side)
+            def _(i, part=part):
+                u, v = i // side, i % side
+                for w in range(side):
+                    work[u, v, w, part] = (
+                        part_ref[s, u, v, w, part].astype(f32) + core_in[u, v, w, part].astype(f32)
+                    ).astype(bf16)
+
+    def send_one(group):
         sent = []
-        for d in range(1, side):
-            if c % 2 == 0:
-                at = (x + d) % side
-                sent.append(remote(work.at[:, :, at, part], in_one.at[d - 1, :, :, part], (z, y, at)))
-            else:
-                at = (y + d) % side
-                sent.append(remote(work.at[:, at, :, part], in_one.at[d - 1, :, :, part], (z, at, x)))
+        for kind, part in group:
+            for d in range(1, side):
+                at = ((x if kind == 0 else y) + d) % side
+                src, there = (work.at[:, :, at, part], (z, y, at)) if kind == 0 else (work.at[:, at, :, part], (z, at, x))
+                sent.append(remote(src, in_one.at[d - 1, :, :, part], there))
         return sent
 
-    def step_one(c, sent):
-        part = chunks[c]
-        for copy in sent:
-            copy.wait_recv()
-
-        @pl.loop(0, size_z * side)
-        def _(i):
-            u, v = i // side, i % side
-            at = (u, v, x) if c % 2 == 0 else (u, y, v)
-            total = work[at + (part,)].astype(f32)
+    def step_one(group):
+        for kind, part in group:
+            @pl.loop(0, size_z)
+            def _(u, kind=kind, part=part):
+                for v in range(side):
+                    at = (u, v, x) if kind == 0 else (u, y, v)
+                    total = work[at + (part,)].astype(f32)
+                    for d in range(1, side):
+                        total = total + in_one[d - 1, u, v, part].astype(f32)
+                    two[v, u, part] = total.astype(bf16)
+
+        sent = []
+        for kind, part in group:
             for d in range(1, side):
-                total = total + in_one[d - 1, u, v, part].astype(f32)
-            two[v, u, part] = total.astype(bf16)
-
-        sent = []
-        for d in range(1, side):
-            at = ((y if c % 2 == 0 else x) + d) % side
-            there = (z, at, x) if c % 2 == 0 else (z, y, at)
-            sent.append(remote(two.at[at, :, part], in_two.at[d - 1, :, part], there))
+                at = ((y if kind == 0 else x) + d) % side
+                there = (z, at, x) if kind == 0 else (z, y, at)
+                sent.append(remote(two.at[at, :, part], in_two.at[d - 1, :, part], there))
         return sent
 
-    def step_two(c, sent):
-        part = chunks[c]
-        for copy in sent:
-            copy.wait_recv()
-
-        @pl.loop(0, size_z)
-        def _(u):
-            total = two[y if c % 2 == 0 else x, u, part].astype(f32)
-            for d in range(1, side):
-                total = total + in_two[d - 1, u, part].astype(f32)
-            three[u, part] = total.astype(bf16)
+    def step_two(group):
+        for kind, part in group:
+            for u in range(size_z):
+                total = two[y if kind == 0 else x, u, part].astype(f32)
+                for d in range(1, side):
+                    total = total + in_two[d - 1, u, part].astype(f32)
+                three[u, part] = total.astype(bf16)
 
         return [
             remote(three.at[(z + d) % size_z, part], in_three.at[d - 1, part], ((z + d) % size_z, y, x))
-            for d in range(1, size_z)
+            for kind, part in group for d in range(1, size_z)
         ]
 
-    def step_three(c, sent):
-        part = chunks[c]
-        for copy in sent:
-            copy.wait_recv()
-        total = three[z, part].astype(f32)
-        for d in range(1, size_z):
-            total = total + in_three[d - 1, part].astype(f32)
-        total_s[part] = total
-
-    one, again, last = {}, {}, {}
-    for t in range(len(chunks) + 3):
-        if t < len(chunks):
-            one[t] = step_core(t)
-        if 0 <= t - 1 < len(chunks):
-            again[t - 1] = step_one(t - 1, one[t - 1])
-        if 0 <= t - 2 < len(chunks):
-            last[t - 2] = step_two(t - 2, again[t - 2])
-        if 0 <= t - 3 < len(chunks):
-            step_three(t - 3, last[t - 3])
+    def step_three(group):
+        for kind, part in group:
+            total = three[z, part].astype(f32)
+            for d in range(1, size_z):
+                total = total + in_three[d - 1, part].astype(f32)
+            total_s[part] = total
+
+    step_core(groups[0])
+    one, again, last = {0: send_one(groups[0])}, {}, {}
+    for t in range(len(groups) + 2):
+        if t + 1 < len(groups):
+            step_core(groups[t + 1])
+        if t < len(groups):
+            for copy in one[t]:
+                copy.wait_recv()
+            if t + 1 < len(groups):
+                one[t + 1] = send_one(groups[t + 1])
+            again[t] = step_one(groups[t])
+        if 0 <= t - 1 < len(groups):
+            for copy in again[t - 1]:
+                copy.wait_recv()
+            last[t - 1] = step_two(groups[t - 1])
+        if 0 <= t - 2 < len(groups):
+            for copy in last[t - 2]:
+                copy.wait_recv()
+            step_three(groups[t - 2])
     if len(outs) == 1:
         outs[0][...] = total_s[...]
     else:
@@ -358,7 +373,7 @@
 def scatter(dims, partials, rows_pair, out_shapes):
     rows, width = partials.shape[-2:]
     size_z, side, _ = dims
-    parts = len(row_chunks(rows))
+    parts = part_count(row_groups(rows, SCATTER_WEIGHTS))
     across = max(parts * ((size_z - 1) + 2 * (side - 1)), 1)
     more = max(side - 1, 1)
     vmem = pl.BlockSpec(memory_space=pltpu.VMEM)
@@ -419,7 +434,7 @@
     )
 
 
-def layers_kernel(seq, per, ff_per, rows_ref, cot_ref, *refs):
+def layer_steps(dims, seq, per, ff_per, rows_ref, cot_ref, refs):
     fast = per is not None
     if fast:
         blocks_ref, out_ref, parts_ref, w_s, tail_s, f_s = refs[:6]
@@ -431,10 +446,15 @@
     kinds = w_s.shape[1]
     down_at = kinds * per if fast else 0
 
+    def at_rank(e, k):
+        _, size_y, size_x = dims
+        return e, k // (size_y * size_x), (k // size_x) % size_y, k % size_x
+
     def down_part(e, c):
         if fast:
             group = width // ff_per
-            return blocks_ref[e, c * group:(c + 1) * group, down_at:down_at + ff_per].reshape(width, width)
+            rows_of = pl.ds(down_at, ff_per)
+            return jnp.concatenate([blocks_ref[at_rank(e, c * group + i) + (rows_of,)] for i in range(group)], axis=0)
         return down_all[e, c * width:(c + 1) * width]
 
     def keep_grad(e, kind, value):
@@ -447,27 +467,26 @@
         if fast:
             group = width // ff_per
             for i in range(group):
-                parts_ref[e, c * group + i, down_at:down_at + ff_per] = value[i * ff_per:(i + 1) * ff_per].astype(bf16)
+                parts_ref[at_rank(e, c * group + i) + (pl.ds(down_at, ff_per),)] = value[i * ff_per:(i + 1) * ff_per].astype(bf16)
         else:
             gdown_ref[e, c * width:(c + 1) * width] = value.astype(bf16)
 
-    if fast:
-        count = blocks_ref.shape[1]
-        for e in range(2):
-            tail_s[e] = jnp.zeros(tail_s.shape[1:], f32)
-
-            @pl.loop(0, count // 2)
-            def _(m, e=e):
-                left = blocks_ref[e, 2 * m, 0:down_at].astype(f32)
-                right = blocks_ref[e, 2 * m + 1, 0:down_at].astype(f32)
-                at = pl.ds(pl.multiple_of(2 * per * m, 2 * per), 2 * per)
-                for kind in range(kinds):
-                    piece = slice(kind * per, (kind + 1) * per)
-                    w_s[e, kind, at] = jnp.concatenate([left[piece], right[piece]], axis=0).astype(bf16)
-                tail_s[e] += (
-                    blocks_ref[e, 2 * m, down_at + ff_per:].astype(f32)
-                    + blocks_ref[e, 2 * m + 1, down_at + ff_per:].astype(f32)
-                )
+    def prepare(e):
+        count = dims[0] * dims[1] * dims[2]
+        tail_s[e] = jnp.zeros(tail_s.shape[1:], f32)
+
+        @pl.loop(0, count // 2)
+        def _(m):
+            first, second = at_rank(e, 2 * m), at_rank(e, 2 * m + 1)
+            top, rest = pl.ds(0, down_at), pl.ds(down_at + ff_per, 16)
+            left = blocks_ref[first + (top,)].astype(f32)
+            right = blocks_ref[second + (top,)].astype(f32)
+            at = pl.ds(pl.multiple_of(2 * per * m, 2 * per), 2 * per)
+            for kind in range(kinds):
+                piece = slice(kind * per, (kind + 1) * per)
+                w_s[e, kind, at] = jnp.concatenate([left[piece], right[piece]], axis=0).astype(bf16)
+            tail_s[e] += blocks_ref[first + (rest,)].astype(f32) + blocks_ref[second + (rest,)].astype(f32)
+
     pairs = width // PAIR
     lane = lax.broadcasted_iota(jnp.int32, (rows, PAIR), 1)
     low_half = lane < HEAD_DIM
@@ -477,10 +496,9 @@
     def halves(values):
         return jnp.where(low_half, values, zero), jnp.where(low_half, zero, values)
 
-    h_s[0] = rows_ref[...].astype(f32)
-
-    @pl.loop(0, 2)
-    def _(e):
+    def forward(e):
+        if e == 0:
+            h_s[0] = rows_ref[...].astype(f32)
         vec = tail_s[e, 0:8]
         bias = tail_s[e, 8:16]
         h = h_s[e]
@@ -521,13 +539,12 @@
             total = total + mm(g_s[e, :, c * width:(c + 1) * width], down_part(e, c))
         result = total.astype(bf16)
         out_ref[0] = result
-        h_s[1] = jnp.where(e == 0, result.astype(f32), h_s[1])
-
-    dy_s[...] = cot_ref[...].astype(f32)
-
-    @pl.loop(0, 2)
-    def _(step):
-        e = 1 - step
+        if e == 0:
+            h_s[1] = result.astype(f32)
+
+    def backward(e):
+        if e == 1:
+            dy_s[...] = cot_ref[...].astype(f32)
         vec = tail_s[e, 0:8]
         dy = dy_s[...]
         dm = dy.astype(bf16)
@@ -589,52 +606,363 @@
         if not fast:
             gtail_ref[e] = gt_s[...]
         else:
-            @pl.loop(0, parts_ref.shape[1])
+            @pl.loop(0, dims[0] * dims[1] * dims[2])
             def _(k):
                 at = pl.ds(pl.multiple_of(per * k, per), per)
+                block = at_rank(e, k)
                 for kind in range(0, kinds, 2):
                     both = jnp.concatenate([f_s[kind, at], f_s[kind + 1, at]], axis=0)
-                    parts_ref[e, k, kind * per:(kind + 2) * per] = both.astype(bf16)
-                parts_ref[e, k, down_at + ff_per:] = gt_s[...].astype(bf16)
-
-
-def run_layers(seq, per, ff_per, rows, cot, weights, kinds, ff):
+                    parts_ref[block + (pl.ds(kind * per, 2 * per),)] = both.astype(bf16)
+                parts_ref[block + (pl.ds(down_at + ff_per, 16),)] = gt_s[...].astype(bf16)
+
+    return prepare, forward, backward
+
+
+def layers_kernel(seq, rows_ref, cot_ref, *refs):
+    _, forward, backward = layer_steps(None, seq, None, None, rows_ref, cot_ref, refs)
+    forward(0)
+    forward(1)
+    backward(1)
+    backward(0)
+
+
+def layer_scratch(t, width, ff):
+    return [
+        pltpu.VMEM((2, t, width), f32),
+        pltpu.VMEM((2, t, width), bf16),
+        pltpu.VMEM((2, t, 3 * width), bf16),
+        pltpu.VMEM((2, t, width), bf16),
+        pltpu.VMEM((2, t, width), f32),
+        pltpu.VMEM((2, t, width), bf16),
+        pltpu.VMEM((2, t, ff), bf16),
+        pltpu.VMEM((2, t, ff), f32),
+        pltpu.VMEM((2, HEADS, t, t), f32),
+        pltpu.VMEM((t, width), f32),
+        pltpu.VMEM((t, width), f32),
+        pltpu.VMEM((t, 3 * width), bf16),
+        pltpu.VMEM((16, width), f32),
+    ]
+
+
+def run_layers(seq, rows, cot, weights, ff):
     t, width = rows.shape
-    fast = per is not None
     vmem = pl.BlockSpec(memory_space=pltpu.VMEM)
     shape = jax.ShapeDtypeStruct
     outs = [shape((2, t, width), bf16)]
     outs += [shape(item.shape, bf16) for item in weights[:2]]
-    if not fast:
-        outs.append(shape(weights[2].shape, f32))
-    extra = [
-        pltpu.VMEM((2, kinds, width, width), bf16),
-        pltpu.VMEM((2, 16, width), f32),
-        pltpu.VMEM((kinds, width, width), f32),
-    ]
+    outs.append(shape(weights[2].shape, f32))
     return pl.pallas_call(
-        functools.partial(layers_kernel, seq, per, ff_per),
+        functools.partial(layers_kernel, seq),
         out_shape=tuple(outs),
         in_specs=[vmem] * (2 + len(weights)),
         out_specs=(vmem,) * len(outs),
-        scratch_shapes=(extra if fast else []) + [
-            pltpu.VMEM((2, t, width), f32),
-            pltpu.VMEM((2, t, width), bf16),
-            pltpu.VMEM((2, t, 3 * width), bf16),
-            pltpu.VMEM((2, t, width), bf16),
-            pltpu.VMEM((2, t, width), f32),
-            pltpu.VMEM((2, t, width), bf16),
-            pltpu.VMEM((2, t, ff), bf16),
-            pltpu.VMEM((2, t, ff), f32),
-            pltpu.VMEM((2, HEADS, t, t), f32),
-            pltpu.VMEM((t, width), f32),
-            pltpu.VMEM((t, width), f32),
-            pltpu.VMEM((t, 3 * width), bf16),
-            pltpu.VMEM((16, width), f32),
-        ],
+        scratch_shapes=layer_scratch(t, width, ff),
         compiler_params=pltpu.CompilerParams(vmem_limit_bytes=VMEM_BYTES),
         name="two_layers",
     )(rows, cot, *weights)
+
+
+def whole_kernel(dims, seq, per, ff_per, *refs):
+    (vec_ref, bias_ref, qkv_ref, wo_ref, up_ref, down_ref, img_ref,
+     qkv_out, wo_out, up_out, down_out, tail_out, ends_out) = refs[:13]
+    (shard_ref, io, blocks, parts, pair, core_in, work, in_one, two, in_two, three, in_three, total_s) = refs[13:26]
+    img_sems, end_sems, g_send, g_recv, gc_send, gc_recv, send_sems, recv_sems, core_send, core_recv = refs[26:36]
+    layer_refs = refs[36:]
+    size_z, side, _ = dims
+    s = lax.axis_index("section")
+    z, y, x = place(dims)
+    build_shard(dims, vec_ref, bias_ref, qkv_ref, wo_ref, up_ref, down_ref, shard_ref)
+    rows, width = shard_ref.shape
+    prepare, forward, backward = layer_steps(
+        dims, seq, per, ff_per, io.at[0], io.at[1], (blocks, pair, parts) + layer_refs
+    )
+    every = slice(None)
+    io[s] = img_ref[s]
+    blocks[s, z, y, x] = shard_ref[...]
+    waiting = []
+    counter = [0, 0, 0]
+
+    def chips(which, sends, recvs, src, dst, there):
+        slot = counter[which]
+        counter[which] += 1
+        copy = pltpu.make_async_remote_copy(
+            src_ref=src, dst_ref=dst, send_sem=sends.at[slot], recv_sem=recvs.at[slot],
+            device_id={"dp": rank(dims, *there)}, device_id_type=MESH,
+        )
+        waiting.append(copy)
+        return copy
+
+    def cores(src, dst, send, recv):
+        return pltpu.make_async_remote_copy(
+            src_ref=src, dst_ref=dst, send_sem=send, recv_sem=recv, device_id={"section": 1 - s}, device_id_type=MESH,
+        )
+
+    def to_core(*at):
+        slot = counter[1]
+        counter[1] += 1
+        mine, other = blocks.at[(s,) + at], blocks.at[(1 - s,) + at]
+        sent = cores(mine, mine, gc_send.at[slot], gc_recv.at[slot])
+        waiting.append(sent)
+        return sent, cores(other, other, gc_send.at[slot], gc_recv.at[slot])
+
+    groups = row_groups(rows, GATHER_WEIGHTS)
+    flat = [item for group in groups for item in group]
+    first, second, third = [], [], []
+    for kind, part in flat:
+        first.append([
+            (chips(0, g_send, g_recv, shard_ref.at[part], blocks.at[s, z, y, x, part], ((z + d) % size_z, y, x)),
+             to_core((z - d + size_z) % size_z, y, x, part))
+            for d in range(1, size_z)
+        ])
+    for kind, part in flat:
+        piece = blocks.at[s, every, y, x, part]
+        hops = []
+        for d in range(1, side):
+            there = (z, (y + d) % side, x) if kind == 0 else (z, y, (x + d) % side)
+            at = ((y if kind == 0 else x) - d + side) % side
+            hops.append((chips(0, g_send, g_recv, piece, piece, there),
+                         to_core(*((every, at, x, part) if kind == 0 else (every, y, at, part)))))
+        second.append(hops)
+    for kind, part in flat:
+        piece = blocks.at[s, every, every, x, part] if kind == 0 else blocks.at[s, every, y, every, part]
+        hops = []
+        for d in range(1, side):
+            there = (z, y, (x + d) % side) if kind == 0 else (z, (y + d) % side, x)
+            at = ((x if kind == 0 else y) - d + side) % side
+            hops.append((chips(0, g_send, g_recv, piece, piece, there),
+                         to_core(*((every, every, at, part) if kind == 0 else (every, at, every, part)))))
+        third.append(hops)
+    own = to_core(z, y, x)
+    image = cores(img_ref.at[1 - s], io.at[s], img_sems.at[0], img_sems.at[1])
+    image_in = cores(img_ref.at[1 - s], io.at[1 - s], img_sems.at[0], img_sems.at[1])
+
+    def begin(hops):
+        for copy, _ in hops:
+            copy.start()
+
+    def pass_on(hops):
+        for copy, (sent, _) in hops:
+            copy.wait_recv()
+            sent.start()
+
+    def arrive(hops):
+        for _, (_, got) in hops:
+            got.wait_recv()
+
+    def scatter_copies():
+        cut = [item for group in row_groups(rows, SCATTER_WEIGHTS) for item in group]
+        out = []
+        for slot, (kind, part) in enumerate(cut):
+            core = cores(parts.at[1 - s, :, :, :, part], core_in.at[:, :, :, part], core_send.at[slot], core_recv.at[slot])
+            one, again, last = [], [], []
+            for d in range(1, side):
+                at = ((x if kind == 0 else y) + d) % side
+                src, there = (work.at[:, :, at, part], (z, y, at)) if kind == 0 else (work.at[:, at, :, part], (z, at, x))
+                one.append(chips(2, send_sems, recv_sems, src, in_one.at[d - 1, :, :, part], there))
+            for d in range(1, side):
+                at = ((y if kind == 0 else x) + d) % side
+                there = (z, at, x) if kind == 0 else (z, y, at)
+                again.append(chips(2, send_sems, recv_sems, two.at[at, :, part], in_two.at[d - 1, :, part], there))
+            for d in range(1, size_z):
+                at = (z + d) % size_z
+                last.append(chips(2, send_sems, recv_sems, three.at[at, part], in_three.at[d - 1, part], (at, y, x)))
+            waiting.append(core)
+            out.append((kind, part, core, one, again, last))
+        return out
+
+    cut = scatter_copies()
+
+    def start_cores():
+        for _, _, core, _, _, _ in cut:
+            core.start()
+
+    def add_cores():
+        for kind, part, core, one, _, _ in cut:
+            core.wait_recv()
+
+            @pl.loop(0, size_z * side)
+            def _(i, part=part):
+                u, v = i // side, i % side
+                for w in range(side):
+                    work[u, v, w, part] = (
+                        parts[s, u, v, w, part].astype(f32) + core_in[u, v, w, part].astype(f32)
+                    ).astype(bf16)
+
+            for copy in one:
+                copy.start()
+
+    def step_one(item):
+        kind, part, _, one, again, _ = item
+        for copy in one:
+            copy.wait_recv()
+
+        @pl.loop(0, size_z)
+        def _(u):
+            for v in range(side):
+                at = (u, v, x) if kind == 0 else (u, y, v)
+                total = work[at + (part,)].astype(f32)
+                for d in range(1, side):
+                    total = total + in_one[d - 1, u, v, part].astype(f32)
+                two[v, u, part] = total.astype(bf16)
+
+        for copy in again:
+            copy.start()
+
+    def step_two(item):
+        kind, part, _, _, again, last = item
+        for copy in again:
+            copy.wait_recv()
+        for u in range(size_z):
+            total = two[y if kind == 0 else x, u, part].astype(f32)
+            for d in range(1, side):
+                total = total + in_two[d - 1, u, part].astype(f32)
+            three[u, part] = total.astype(bf16)
+        for copy in last:
+            copy.start()
+
+    def step_three(item):
+        _, part, _, _, _, last = item
+        for copy in last:
+            copy.wait_recv()
+        total = three[z, part].astype(f32)
+        for d in range(1, size_z):
+            total = total + in_three[d - 1, part].astype(f32)
+        total_s[part] = total
+
+    greet(dims, s, z, y, x)
+
+    @pl.when(s == 1)
+    def _():
+        for hops in first:
+            arrive(hops)
+
+    for hops in first:
+        begin(hops)
+    image.start()
+    own[0].start()
+    for near, far in zip(first, second):
+        pass_on(near)
+        begin(far)
+    for near, far in zip(second, third):
+        pass_on(near)
+        begin(far)
+
+    def finish():
+        for hops in third:
+            pass_on(hops)
+
+    @pl.when(s == 0)
+    def _():
+        finish()
+
+    @pl.when(s == 1)
+    def _():
+        own[1].wait_recv()
+        for hops in second + third:
+            arrive(hops)
+
+    image_in.wait_recv()
+    prepare(0)
+    forward(0)
+
+    @pl.when(s == 1)
+    def _():
+        finish()
+
+    @pl.when(s == 0)
+    def _():
+        own[1].wait_recv()
+        for hops in first + second + third:
+            arrive(hops)
+
+    prepare(1)
+    forward(1)
+    backward(1)
+
+    @pl.when(s == 0)
+    def _():
+        start_cores()
+
+    @pl.when(s == 1)
+    def _():
+        add_cores()
+
+    backward(0)
+    end = cores(pair.at[s], ends_out.at[s], end_sems.at[0], end_sems.at[1])
+    end_in = cores(pair.at[s], ends_out.at[1 - s], end_sems.at[0], end_sems.at[1])
+
+    @pl.when(s == 1)
+    def _():
+        start_cores()
+
+    @pl.when(s == 0)
+    def _():
+        add_cores()
+
+    end.start()
+    ends_out[s] = pair[1 - s]
+    for step in (step_one, step_two, step_three):
+        for item in cut:
+            step(item)
+    spots = [(qkv_out, i) for i in range(3)] + [(wo_out, 0)] + [(up_out, i) for i in range(up_out.shape[1] // width)]
+    for i, (ref, j) in enumerate(spots):
+        ref[:, j * width:(j + 1) * width] = total_s[i * per:(i + 1) * per]
+    top = len(spots) * per
+    down_out[...] = total_s[top:top + ff_per]
+    tail_out[...] = total_s[top + ff_per:]
+    for copy in waiting:
+        copy.wait_send()
+    image.wait_send()
+    end.wait_send()
+    end_in.wait_recv()
+
+
+def run_whole(dims, seq, sources, images, rows, kinds, ff):
+    per, width = sources[3].shape
+    ff_per = sources[5].shape[0]
+    t = images.shape[1]
+    size_z, side, _ = dims
+    hops = (size_z - 1) + 2 * (side - 1)
+    g_parts = part_count(row_groups(rows, GATHER_WEIGHTS))
+    s_parts = part_count(row_groups(rows, SCATTER_WEIGHTS))
+    more = max(side - 1, 1)
+    vmem = pl.BlockSpec(memory_space=pltpu.VMEM)
+    dma = pltpu.SemaphoreType.DMA
+    shape = jax.ShapeDtypeStruct
+    return pl.pallas_call(
+        functools.partial(whole_kernel, dims, seq, per, ff_per),
+        out_shape=(
+            shape((per, 3 * width), f32), shape((per, width), f32), shape((per, ff), f32), shape((ff_per, width), f32),
+            shape((16, width), f32), shape(images.shape, bf16),
+        ),
+        in_specs=[vmem] * 7,
+        out_specs=(vmem,) * 6,
+        scratch_shapes=[
+            pltpu.VMEM((rows, width), bf16),
+            pltpu.VMEM((2, t, width), bf16),
+            pltpu.VMEM((2,) + dims + (rows, width), bf16),
+            pltpu.VMEM((2,) + dims + (rows, width), bf16),
+            pltpu.VMEM((2, t, width), bf16),
+            pltpu.VMEM(dims + (rows, width), bf16),
+            pltpu.VMEM(dims + (rows, width), bf16),
+            pltpu.VMEM((more, size_z, side, rows, width), bf16),
+            pltpu.VMEM((side, size_z, rows, width), bf16),
+            pltpu.VMEM((more, size_z, rows, width), bf16),
+            pltpu.VMEM((size_z, rows, width), bf16),
+            pltpu.VMEM((max(size_z - 1, 1), rows, width), bf16),
+            pltpu.VMEM((rows, width), f32),
+            dma((2,)), dma((2,)),
+            dma((max(g_parts * hops, 1),)), dma((max(g_parts * hops, 1),)),
+            dma((g_parts * hops + 1,)), dma((g_parts * hops + 1,)),
+            dma((max(s_parts * hops, 1),)), dma((max(s_parts * hops, 1),)),
+            dma((s_parts,)), dma((s_parts,)),
+            pltpu.VMEM((2, kinds, width, width), bf16),
+            pltpu.VMEM((2, 16, width), f32),
+            pltpu.VMEM((kinds, width, width), f32),
+        ] + layer_scratch(t, width, ff),
+        compiler_params=pltpu.CompilerParams(collective_id=2, has_side_effects=True, vmem_limit_bytes=VMEM_BYTES),
+        name="whole_step",
+    )(*sources, images)
 
 
 def pack(count, pieces, down, tail):
@@ -678,37 +1006,29 @@
 
     if fast:
         sources = (vectors[0], up_bias, w_qkv[0], w_out[0], w_up[0], w_down[0])
+        fqkv, fwo, fup, fdown, ftail, ends = run_whole(dims, seq, sources, padded, rows, kinds, ff)
     else:
         tail = build_tail(me, vectors[0], up_bias, ups, width)
         pieces = jnp.concatenate([columns(w_qkv[0]), w_out[0][None], columns(w_up[0])])
         sources = (pack(1, pieces, w_down[0], tail)[0],)
-    blocks, other = gather(dims, fast, sources, padded, rows, width)
-    blocks = blocks.reshape(2, count, rows, width)
-    own = lax.dynamic_index_in_dim(padded, section_id, 0, keepdims=False)
-    x_rows = jnp.where(is_first, own, other)
-    cot = jnp.where(is_first, other, own)
-    if fast:
-        pair, partials = run_layers(seq, per, ff_per, x_rows, cot, (blocks,), kinds, ff)
-    else:
-        pieces, down, tails = unpack(blocks, kinds, per, ff_per)
+        blocks, other = gather(dims, False, sources, padded, rows, width)
+        own = lax.dynamic_index_in_dim(padded, section_id, 0, keepdims=False)
+        x_rows = jnp.where(is_first, own, other)
+        cot = jnp.where(is_first, other, own)
+        pieces, down, tails = unpack(blocks.reshape(2, count, rows, width), kinds, per, ff_per)
         tail = jnp.sum(tails.astype(f32), axis=1)
-        pair, gpieces, gdown, gtail = run_layers(seq, None, None, x_rows, cot, (pieces, down, tail), kinds, ff)
-        partials = pack(count, gpieces, gdown, gtail)
-    partials = partials.reshape((2,) + dims + (rows, width))
-    if fast:
-        shapes = ((per, 3 * width), (per, width), (per, ff), (ff_per, width), (16, width))
-        fqkv, fwo, fup, fdown, ftail, got = scatter(dims, partials, pair, shapes)
-    else:
+        pair, gpieces, gdown, gtail = run_layers(seq, x_rows, cot, (pieces, down, tail), ff)
+        partials = pack(count, gpieces, gdown, gtail).reshape((2,) + dims + (rows, width))
         total, got = scatter(dims, partials, pair, ((rows, width),))
         pieces, fdown, ftail = unpack(total[None], kinds, per, ff_per)
         ftail = ftail[0]
         fqkv = jnp.moveaxis(pieces[:3], 0, 1).reshape(per, 3 * width)
         fwo = pieces[3]
         fup = jnp.moveaxis(pieces[4:], 0, 1).reshape(per, ff)
+        ends = jnp.stack([jnp.where(is_first, pair[1], got), jnp.where(is_first, got, pair[0])])
     fvec = lax.dynamic_slice_in_dim(ftail[:vec_rows], me * per, per, 1)
     fbias = lax.dynamic_slice_in_dim(ftail[8:8 + ups].reshape(-1), me * ff_per, ff_per, 0)
-    ends = jnp.stack([jnp.where(is_first, pair[1], got), jnp.where(is_first, got, pair[0])])[None, :, :seq]
-    return ends, fvec[None], fbias[None], fqkv[None], fwo[None], fup[None], fdown[None]
+    return ends[None, :, :seq], fvec[None], fbias[None], fqkv[None], fwo[None], fup[None], fdown[None]
 
 
 def solution(mesh):

time: 154 us -> 117 us (0.76); the launches traced: 152 us -> 117 us
  Pallas kernels: 137 us -> 108 us
  local copies, waits for them, and re-layouts: 11.5 us -> 7.98 us
  other arithmetic: 2.67 us -> 0 us
    pallas_call x3 -> x1, Pallas kernels: 137 us -> 108 us  [run_whole(): pl.pallas_call(functools.partial(whole_kernel, dims, seq, per, ff_per), o...]
    unnamed x8 -> x16, local copies, waits for them, and re-layouts: 8.05 us -> 4.97 us
    select_n x1 -> x0, other arithmetic: 1.69 us -> none  [shards(): cot = jnp.where(is_first, other, own)]
where the time goes in v3:
time: 117 us
  Pallas kernels  108 us (92%)
  local copies, waits for them, and re-layouts  7.98 us (7%)
    pallas_call x1, Pallas kernels, run_whole(): pl.pallas_call(functools.partial(whole_kernel, dims, seq, per, ff_per), o...  108 us
    unnamed x16, local copies, waits for them, and re-layouts  4.97 us

profile of v3, /device:TPU:0, one launch (start us, length us, event | category | flops | bytes accessed | tf_op | source)
XLA Modules:
  0.0 116.7 jit_solution(7658813257974224817)
XLA Ops:
  0.6 1.0 copy.17
  1.6 0.7 pad.4.refs_6_
  2.4 108.0 %whole_step.1 = (f32[24,1152]{1,0:T(8,128)}, f32[24,384]{1,0:T(8,128)}, f32[24,1536]{1,0:T(8,128)}, f32[96,384]{1,0:T(8,128)}, f32[16,384]{1,0:T(8,128)}, /*index=5*/bf16[2,208,384]{2,1,0:T(8,128)(2,1)}) custom-call(bf16[8,24]{1,0:T(8,128)(2,1)} %bitcast.27, bf16[1,96]{1,0:T(2,128)(2,1)} %refs_1_.1, bf16[24,1152]{1,0:T(8,128)(2,1)} %bitcast.24, ...), custom_call_target="tpu_custom_call" | custom-call | tf_op jit(solution)/shard_map/whole_step/pallas_call | solution.py:932
  110.4 1.0 slice_bitcast_fusion
  111.4 0.0 copy-start.4
  111.4 0.0 copy-start.2
  111.5 1.0 copy.15
  112.4 0.0 copy-done.4
  112.4 0.7 dynamic-slice_bitcast_fusion
  113.1 0.6 dynamic-slice_bitcast_fusion.1
  113.7 0.0 copy-done.2
  113.7 0.0 copy-start.3
  113.7 0.0 copy-start.1
  113.7 0.6 copy.22
  114.3 0.1 copy-done.3
  114.4 0.6 copy.23
  115.1 0.0 copy-done.1
  115.1 0.0 copy-start
  115.1 0.7 copy.24
  115.7 0.3 copy-done
  116.0 0.7 copy.25
  (3 shorter events, 0.0 us)
Async XLA Ops:
  111.4 1.0 copy-start.4
  111.4 2.2 %copy-start.2 = (f32[24,1152]{1,0:T(8,128)S(1)}, f32[24,1152]{1,0:T(8,128)}, u32[]{:S(2)}) copy-start(f32[24,1152]{1,0:T(8,128)} %get-tuple-element.15) | copy-start | bytes 331780
  113.7 0.8 copy-start.3
  113.7 1.4 %copy-start.1 = (f32[24,1536]{1,0:T(8,128)S(1)}, f32[24,1536]{1,0:T(8,128)}, u32[]{:S(2)}) copy-start(f32[24,1536]{1,0:T(8,128)} %get-tuple-element.17) | copy-start | bytes 442372
  115.1 1.0 copy-start
